TPU v7x, 256 devices: a whole 4x4x8 slice. The times are simulated.
256 devices in a mesh: gy: 64 (over z, y, core), gz: 4 (over x).
Axes of the slice: x: 4, y: 4, z: 8, core: 2. Of those that a mesh axis runs over, the one named last changes fastest.
Arguments:
- field: bfloat16 [32, 8, 1024, 1024], P(None, None, 'gy', 'gz'), may hold values from -6 to 6
- spectral_weight: bfloat16 [256, 32, 1024], P('gy', 'gz'), may hold values from -1 to 1
- point_weight: bfloat16 [32, 32], replicated, may hold values from -1 to 1
- bias: float32 [32], replicated, may hold values from -3 to 3
Outputs:
- layer_out: bfloat16 [32, 8, 1024, 1024], P(None, None, 'gy', 'gz')
All inputs are finite; a program needn't handle non-finite values.
Results may differ from a plain program's by a relative error of at most 0.013.
Values may be sent and summed in bfloat16 or wider, within the bound.
No kernel may reach another device: no remote copies, remote signals or barrier semaphores. Data moves between devices by JAX's collectives and lax.ppermute only.
A program may use at most 64 MiB of HBM per device.

v0:
```python
import math

import jax
import jax.numpy as jnp
from jax import lax
from jax.sharding import PartitionSpec as P

KY = 32
KZ = 32


def basis(count, length, start, size, norm):
    modes = jnp.arange(count, dtype=jnp.float32)[:, None]
    spots = (start + lax.iota(jnp.int32, size)).astype(jnp.float32)[None, :]
    value = norm * jnp.cos(jnp.pi * modes * (spots + 0.5) / length)
    return jnp.where(modes == 0, value * math.sqrt(0.5), value)


def shards(field, spectral_weight, point_weight, bias):
    highest = lax.Precision.HIGHEST
    chans, planes, rows, depth = field.shape
    rows_devs = lax.axis_size("gy")
    depth_devs = lax.axis_size("gz")
    total_rows = rows * rows_devs
    total_depth = depth * depth_devs
    row_start = lax.axis_index("gy") * rows
    depth_start = lax.axis_index("gz") * depth
    analysis_z = basis(KZ, total_depth, depth_start, depth, math.sqrt(2.0 / total_depth)).astype(
        jnp.bfloat16
    )
    analysis_y = basis(KY, total_rows, row_start, rows, math.sqrt(2.0 / total_rows))
    analysis_x = basis(planes, planes, 0, planes, math.sqrt(2.0 / planes))
    first_share = planes * KY // rows_devs
    depth_share = KZ // depth_devs
    weight = spectral_weight.reshape(first_share, depth_share, chans, chans).astype(jnp.float32)
    projected = jnp.einsum("cxyz,kz->cxyk", field, analysis_z, preferred_element_type=jnp.float32)
    partial_value = jnp.einsum("cxyk,jy->cxjk", projected, analysis_y, precision=highest)
    partial_value = jnp.einsum("cxjk,ix->cijk", partial_value, analysis_x, precision=highest)
    partial_value = partial_value.reshape(chans, planes * KY, KZ)
    reduced = lax.psum_scatter(partial_value, "gy", scatter_dimension=1, tiled=True)
    owned = lax.psum_scatter(reduced, "gz", scatter_dimension=2, tiled=True)
    mixed = jnp.einsum("cab,abco->oab", owned, weight, precision=highest).astype(jnp.bfloat16)
    widened = lax.all_gather(mixed, "gz", axis=2, tiled=True)
    full_modes = lax.all_gather(widened, "gy", axis=1, tiled=True)
    modes = full_modes.astype(jnp.float32).reshape(chans, planes, KY, KZ)
    synth_x = basis(planes, planes, 0, planes, math.sqrt(2.0 / planes))
    synth_y = basis(KY, total_rows, row_start, rows, math.sqrt(2.0 / KY))
    synth_z = basis(KZ, total_depth, depth_start, depth, math.sqrt(2.0 / KZ))
    spatial = jnp.einsum("cijk,ix->cxjk", modes, synth_x, precision=highest)
    spatial = jnp.einsum("cxjk,jy->cxyk", spatial, synth_y, precision=highest)
    spatial = jnp.einsum("cxyk,kz->cxyz", spatial, synth_z, precision=highest)
    local = jnp.einsum("cxyz,co->oxyz", field, point_weight, preferred_element_type=jnp.float32)
    total = spatial + local + bias[:, None, None, None]
    return jax.nn.gelu(total, approximate=True).astype(jnp.bfloat16)


def solution(mesh):
    return jax.shard_map(
        shards,
        mesh=mesh,
        in_specs=(P(None, None, "gy", "gz"), P("gy", "gz", None), P(), P()),
        out_specs=P(None, None, "gy", "gz"),
        check_vma=False,
    )
```

profile of v0, /device:TPU:1, one launch (start us, length us, event | category | flops | bytes accessed | tf_op | source)
XLA Modules:
  0.0 280.8 jit_solution(15651090024783393831)
XLA Ops:
  6.5 0.0 copy-start
  6.5 0.0 reduce-scatter.2.cloned.1.call-start
  6.6 1.5 copy-done
  8.1 3.2 %fusion.22 = f32[32,8,16,32]{0,3,2,1:T(8,128)} fusion(bf16[32,8,16,256]{3,2,1,0:T(8,128)(2,1)S(1)} %copy-done, f32[256]{0:T(256)S(1)} %convert_add_fusion, f32[32]{0:T(128)S(1)} %iota_multiply_fusion.1, pred[32]{0:T(512)(128)(4,1)S(1)} %iota_compare_fusion.1), kind=kOutput, calls=%fused_computation.24 | convolution fusion | flops 67158016 | bytes 2622624 | tf_op jit(solution)/shard_map/cxyz,kz->cxyk/dot_general | solution.py:36
  11.3 3.7 %copy.35 = f32[32,8,16,32]{3,2,1,0:T(8,128)} copy(f32[32,8,16,32]{0,3,2,1:T(8,128)} %fusion.22) | data formatting | bytes 1048576 | tf_op jit(solution)/shard_map/cxyz,kz->cxyk/dot_general | solution.py:36
  15.0 5.3 %convolution_bitcast_fusion.1 = f32[32,8,32,32]{3,2,1,0:T(8,128)S(1)} fusion(f32[32,8,16,32]{3,2,1,0:T(8,128)} %copy.35, f32[16]{0:T(128)S(1)} %convert_add_fusion.2, f32[32]{0:T(128)S(1)} %iota_multiply_fusion.1, pred[32]{0:T(512)(128)(4,1)S(1)} %iota_compare_fusion.1), kind=kOutput, calls=%fused_computation.17 | convolution fusion | flops 50334208 | bytes 1573088 | tf_op jit(solution)/shard_map/cxyk,jy->cxjk/dot_general | solution.py:37
  20.4 5.9 %fusion.13 = f32[32,8,32,32]{3,1,2,0:T(8,128)S(1)} fusion(f32[32,8,32,32]{3,2,1,0:T(8,128)S(1)} %convolution_bitcast_fusion.1, f32[8]{0:T(128)S(1)} %get-tuple-element.5, f32[8]{0:T(128)S(1)} %get-tuple-element.6, pred[8]{0:T(512)(128)(4,1)S(1)} %iota_compare_fusion), kind=kOutput, calls=%fused_computation.15 | convolution fusion | flops 25166144 | bytes 2097224 | tf_op jit(solution)/shard_map/cxjk,ix->cijk/dot_general | solution.py:38
  26.3 4.6 %copy.58 = f32[32,8,32,32]{3,0,2,1:T(8,128)} copy(f32[32,8,32,32]{3,1,2,0:T(8,128)S(1)} %fusion.13) | data formatting | bytes 2097152 | tf_op jit(solution)/shard_map/reshape | solution.py:39
  30.9 0.0 copy-start.2
  30.9 0.0 copy-start.5
  30.9 0.0 copy-start.3
  30.9 0.0 reduce-scatter.2.cloned.1.call-update
  30.9 0.8 copy-done.2
  31.7 0.2 reshape.51
  31.9 0.0 copy-done.5
  31.9 0.6 dynamic-slice
  33.2 0.0 copy-done.3
  33.2 3.3 %fusion.18 = f32[32,8,16,256]{3,0,2,1:T(8,128)} fusion(bf16[32,8,16,256]{3,2,1,0:T(8,128)(2,1)S(1)} %copy-done, bf16[32,32]{1,0:T(8,128)(2,1)S(1)} %copy-done.3), kind=kOutput, calls=%fused_computation.20 | convolution fusion | flops 67108864 | bytes 6293504 | tf_op jit(solution)/shard_map/cxyz,co->oxyz/dot_general | solution.py:52
  36.5 137.2 %reduce-scatter.2.cloned.1.call-done = f32[32,4,32]{2,0,1:T(8,128)} async-done(((f32[32,256,32]{2,0,1:T(8,128)}), f32[32,4,32]{2,0,1:T(8,128)}) %reduce-scatter.2.cloned.1.call-update) | async-done | bytes 16400 | tf_op jit(solution)/shard_map/reduce_scatter | solution.py:40
  173.7 0.9 copy.40
  174.6 13.7 %all-reduce = f32[32,4,32]{0,1,2:T(4,128)S(1)} all-reduce(f32[32,4,32]{0,1,2:T(4,128)S(1)} %copy.40), channel_id=3, replica_groups=mesh['gy'=64,'gz'=4] {'gz'}, use_global_device_ids=true, to_apply=%region_1.2.clone | all-reduce | flops 4096 | bytes 32768
  188.3 0.3 fusion.31
  188.7 9.3 %all_gather.6 = bf16[32,4,32]{0,1,2:T(4,128)(2,1)S(1)} all-gather(bf16[32,4,8]{0,1,2:T(4,128)(2,1)S(1)} %bitcast.59), channel_id=1, replica_groups=mesh['gy'=64,'gz'=4] {'gz'}, dimensions={2}, use_global_device_ids=true | all-gather | bytes 10240 | tf_op jit(solution)/shard_map/all_gather | solution.py:43
  197.9 0.1 copy.41
  198.0 61.5 %all_gather.7 = bf16[32,256,32]{2,0,1:T(8,128)(2,1)S(1)} all-gather(bf16[32,4,32]{2,0,1:T(8,128)(2,1)S(1)} %copy.41), channel_id=1, replica_groups=mesh['gy'=64,'gz'=4] {'gy'}, dimensions={1}, use_global_device_ids=true | all-gather | bytes 532480 | tf_op jit(solution)/shard_map/all_gather | solution.py:44
  259.5 4.0 %convolution_bitcast_fusion = f32[32,8,32,32]{3,1,2,0:T(8,128)S(1)} fusion(bf16[32,8,32,32]{3,0,2,1:T(8,128)(2,1)S(1)} %bitcast.58, f32[8]{0:T(128)S(1)} %get-tuple-element.5, f32[8]{0:T(128)S(1)} %get-tuple-element.6, pred[8]{0:T(512)(128)(4,1)S(1)} %iota_compare_fusion), kind=kOutput, calls=%fused_computation.16 | convolution fusion | flops 25166144 | bytes 1572936 | tf_op jit(solution)/shard_map/cijk,ix->cxjk/dot_general | solution.py:49
  263.5 0.0 copy-start.1
  263.5 0.0 copy-start.4
  263.5 2.7 fusion.9
  266.2 0.0 copy-done.1
  266.2 0.0 copy-done.4
  266.3 7.7 %fusion.7 = bf16[32,8,16,256]{3,2,1,0:T(8,128)(2,1)} fusion(f32[32,8,16,256]{3,0,2,1:T(8,128)S(1)} %copy-done.1, f32[16,32,8,32]{3,0,2,1:T(8,128)S(1)} %fusion.9, f32[32]{0:T(128)S(1)} %copy-done.4, f32[256]{0:T(256)S(1)} %convert_add_fusion, f32[32]{0:T(128)S(1)} %iota_multiply_fusion.1, pred[32]{0:T(512)(128)(4,1)S(1)} %iota_compare_fusion.1), kind=kOutput, calls=%fused_computation.8 | convolution fusion | flops 414228480 | bytes 6817056 | tf_op jit(solution)/shard_map/cxyk,kz->cxyz/dot_general | solution.py:51
  (8 shorter events, 0.1 us)
Async XLA Ops:
  6.5 1.6 copy-start
  6.5 167.2 %reduce-scatter.2.cloned.1.call-start = ((), (), s32[]{:S(2)}) async-start(), calls=%async_computation.1 | async-start | bytes 4259840 | tf_op jit(solution)/shard_map/reduce_scatter | solution.py:40
  30.9 0.8 copy-start.2
  30.9 1.0 copy-start.5
  30.9 2.3 copy-start.3
  263.5 2.8 copy-start.1
  263.5 2.8 copy-start.4
Sparse Core Ops, SparseCore 0:
  31.0 142.6 reduce-scatter.1
where the time goes:
time: 281 us
  waiting for transfers between devices  137 us (49%)
  blocking collectives  84.4 us (30%)
  matrix products  32.4 us (12%)
  between operations  14.2 us (5%)
  local copies, waits for them, and re-layouts  12.5 us (4%)
    reduce_scatter x1, waiting for transfers between devices, shards(): lax.psum_scatter(partial_value, 'gy', scatter_dimension=1, tiled=True)  137 us
    all_gather x1, blocking collectives, shards(): full_modes = lax.all_gather(widened, 'gy', axis=1, tiled=True)  61.5 us
    unnamed x1, blocking collectives  13.7 us
    all_gather x1, blocking collectives, shards(): widened = lax.all_gather(mixed, 'gz', axis=2, tiled=True)  9.26 us
    dot_general x1, matrix products, shards(): spatial = jnp.einsum('cxyk,kz->cxyz', spatial, synth_z, precision=highest)  7.72 us
    dot_general x1, matrix products, shards(): jnp.einsum('cxjk,ix->cijk', partial_value, analysis_x, precision=highest)  5.9 us
  transfers between devices with their start and end apart: 1, of which 1 were waited for; matrix products, arithmetic and copies ran while one was open for 1% of the time, Pallas kernels for 0%

commit v1 on v0

v1 whole, which is shorter than its diff:
```python
import math

import jax
import jax.numpy as jnp
import ml_dtypes
import numpy as np
from jax import lax
from jax.experimental import pallas as pl
from jax.experimental.pallas import tpu as pltpu
from jax.sharding import Mesh
from jax.sharding import PartitionSpec as P

C, X, K, N = 32, 8, 32, 1024
DZ, DY, DC, DX = 8, 4, 2, 4
ROWS = N // (DZ * DY * DC)
DEPTH = N // DX
BF = jnp.bfloat16
F32 = jnp.float32


def cosines(count, length, norm):
    modes = np.arange(count, dtype=np.float64)[:, None]
    spots = np.arange(length, dtype=np.float64)[None, :]
    value = norm * np.cos(np.pi * modes * (spots + 0.5) / length)
    value[0] *= math.sqrt(0.5)
    return value


def tables():
    ax = cosines(X, X, math.sqrt(2.0 / X))
    ay = cosines(K, N, math.sqrt(2.0 / N))
    az = cosines(K, N, math.sqrt(2.0 / N)).astype(ml_dtypes.bfloat16).astype(np.float64)
    sz = cosines(K, N, math.sqrt(2.0 / K))
    kq, kx, i = np.meshgrid(np.arange(4), np.arange(DX), np.arange(X), indexing="ij")
    front = np.zeros((DX, X, DC, 128, DEPTH))
    for core in range(DC):
        k = (kx * 8 + core * 4 + kq).reshape(-1)
        rows = az[k].reshape(128, DX, DEPTH).transpose(1, 0, 2)
        mixx = ax[i.reshape(-1)]
        front[:, :, core] = rows[:, None] * mixx.T[None, :, :, None]
    along = np.zeros((DZ * DY * DC, 32, 32))
    for dev in range(DZ * DY * DC):
        core = dev % 2
        spots = np.concatenate([dev * ROWS + np.arange(ROWS), (dev ^ 1) * ROWS + np.arange(ROWS)])
        octet = np.concatenate([core * 4 + np.arange(4), (1 - core) * 4 + np.arange(4)])
        j = (np.arange(4)[:, None] * 8 + octet[None, :]).reshape(-1)
        along[dev] = ay[j][:, spots].T
    back = np.zeros((DX * DC, 48, DEPTH))
    q2, x2 = np.meshgrid(np.arange(4), np.arange(DX), indexing="ij")
    for chip in range(DX):
        for core in range(DC):
            own = (x2 * 8 + core * 4 + q2).reshape(-1)
            other = (x2 * 8 + (1 - core) * 4 + q2).reshape(-1)
            part = slice(chip * DEPTH, (chip + 1) * DEPTH)
            back[chip * 2 + core, :16] = sz[own][:, part]
            back[chip * 2 + core, 16:32] = sz[other][:, part]
            back[chip * 2 + core, 32:35] = 1.0
    planes = np.zeros((X, 16, 16, X))
    for m in range(16):
        planes[:, m, m, :] = ax.T * math.sqrt(N / K)
    bf = ml_dtypes.bfloat16
    return (
        front.astype(bf),
        along.astype(bf),
        back.astype(bf),
        planes.reshape(128, 128).astype(bf),
    )


def dot(a, b, dims=((1,), (0,))):
    return lax.dot_general(a, b, (dims, ((), ())), preferred_element_type=F32)


def iota(shape, dim):
    return lax.broadcasted_iota(jnp.int32, shape, dim)


def ones_where(condition):
    return jnp.where(condition, 1.0, 0.0).astype(BF)


def tables_kernel(at_ref, along_ref, point_ref, bias_ref, wy_ref, kron_ref, shift_ref, spread_ref):
    p1 = ones_where(
        (iota((512, 32), 0) // 256 == iota((512, 32), 1) // 16)
        & (iota((512, 32), 0) % 16 == iota((512, 32), 1) % 16)
    )
    p2 = ones_where(
        (iota((32, 512), 0) // 8 == iota((32, 512), 1) // 128)
        & (iota((32, 512), 0) % 8 == iota((32, 512), 1) % 8)
    )
    full = dot(dot(p1, along_ref[0]).astype(BF), p2)
    same = (iota((512, 512), 0) // 16) % 16 == (iota((512, 512), 1) // 8) % 16
    wy_ref[...] = jnp.where(same, full, 0.0).astype(BF)
    e1 = ones_where(iota((512, 32), 0) // 16 == iota((512, 32), 1))
    e2 = ones_where(iota((32, 512), 0) == iota((32, 512), 1) // 16)
    wide = dot(dot(e1, point_ref[...], ((1,), (1,))).astype(BF), e2)
    same = iota((512, 512), 0) % 16 == iota((512, 512), 1) % 16
    kron_ref[...] = jnp.where(same, wide, 0.0).astype(BF)
    b = jnp.broadcast_to(bias_ref[...], (16, 32))
    b1 = b.astype(BF).astype(F32)
    b2 = (b - b1).astype(BF).astype(F32)
    b3 = b - b1 - b2
    row = iota((16, 32), 0)
    parts = jnp.where(row == 0, b1, jnp.where(row == 1, b2, jnp.where(row == 2, b3, 0.0)))
    shift_ref[...] = dot(parts.astype(BF), e2).astype(BF)
    spread_ref[...] = ones_where(iota((256, 1024), 0) // 8 == iota((256, 1024), 1) // 32)


def analysis_kernel(at_ref, field_ref, mine_ref, other_ref, own_ref, send_ref, acc0, acc1):
    plane = field_ref[...].reshape(C * ROWS, DEPTH)
    a0 = dot(mine_ref[0, 0, 0], plane, ((1,), (1,)))
    a1 = dot(other_ref[0, 0, 0], plane, ((1,), (1,)))
    step = pl.program_id(0)

    @pl.when(step == 0)
    def _():
        acc0[...] = a0
        acc1[...] = a1

    @pl.when(step > 0)
    def _():
        acc0[...] += a0
        acc1[...] += a1

    @pl.when(step == X - 1)
    def _():
        own_ref[...] = acc0[...].astype(BF)
        send_ref[...] = acc1[...].astype(BF)


def rows_kernel(own_ref, recv_ref, wy_ref, out_ref, scratch):
    for g in range(2):
        half = pl.ds(g * 256, 256)
        lhs = jnp.concatenate([own_ref[:, half], recv_ref[:, half]], axis=1)
        res = dot(lhs, wy_ref[...])
        for kq in range(4):
            for kx in range(4):
                for joct in range(4):
                    start = (kx * 4 + joct) * 64 + g * 4 + kq
                    first = (kq * 4 + kx) * 8
                    scratch[pl.ds(start, 8, stride=8), :] = res[
                        first : first + 8, joct * 128 : (joct + 1) * 128
                    ]
    out_ref[...] = scratch[...].astype(BF)


def mix_kernel(at_ref, parts_ref, weight_ref, peer_ref, spread_ref, out_ref):
    core = at_ref[0]
    s = jnp.sum(parts_ref[...].astype(F32).reshape(128, 8, 128), axis=0)
    row = iota((8, 128), 0)
    turned = pltpu.roll(s, 4, 0)
    s8 = jnp.concatenate([jnp.where(row < 4, s, turned), jnp.where(row < 4, turned, s)], axis=1)
    s64 = jnp.concatenate([s8] * 8, axis=0)
    row = iota((64, 256), 0)
    keep = (iota((64, 256), 1) % 8 == row // 8) & ((row % 8) // 4 == core)
    s64 = jnp.where(keep, s64, 0.0)
    high = s64.astype(BF)
    low = (s64 - high.astype(F32)).astype(BF)
    spread = spread_ref[...]
    wide = dot(high, spread) + dot(low, spread)
    weight = jnp.concatenate(
        [weight_ref[...].astype(F32).reshape(32, 1024), peer_ref[...].astype(F32).reshape(32, 1024)], axis=0
    )
    prod = wide * weight
    total = prod[:, 0:128]
    for part in range(1, 8):
        total = total + prod[:, part * 128 : (part + 1) * 128]
    total = total + pltpu.roll(total, 64, 1)
    total = total + pltpu.roll(total, 32, 1)
    mixed = total.astype(BF)
    q, col = iota((128, 256), 0), iota((128, 256), 1)
    place = ones_where(q == (col // 128) * 16 + (col % 128) // 8)
    placed = dot(mixed, place)
    placed = jnp.where(iota((64, 256), 1) % 8 == iota((64, 256), 0) // 8, placed, 0.0).astype(BF)
    take = ones_where(iota((8, 64), 0) % 4 == iota((8, 64), 1) % 4)
    both = dot(take, placed)
    out = jnp.where(iota((8, 128), 0) < 4, both[:, :128], both[:, 128:])
    out_ref[...] = jnp.broadcast_to(out[None], (128, 8, 128)).reshape(1024, 128).astype(BF)


def modes_kernel(modes_ref, wy_ref, planes_ref, own_ref, send_ref, scratch):
    scratch[...] = modes_ref[...].astype(F32)
    for g in range(2):
        cols = []
        for joct in range(4):
            pieces = []
            for kq in range(4):
                for kx in range(4):
                    start = (kx * 4 + joct) * 64 + g * 4 + kq
                    pieces.append(scratch[pl.ds(start, 8, stride=8), :])
            cols.append(jnp.concatenate(pieces, axis=0))
        lhs = jnp.concatenate(cols, axis=1).astype(BF)
        res = dot(lhs, wy_ref[...], ((1,), (1,))).astype(BF)
        res = dot(planes_ref[...], res).astype(BF)
        half = pl.ds(g * 256, 256)
        own_ref[:, half] = res[:, :256]
        send_ref[:, half] = res[:, 256:]


def grid_kernel(at_ref, field_ref, kron_ref, own_ref, recv_ref, shift_ref, back_ref, out_ref):
    plane = field_ref[...].reshape(C * ROWS, DEPTH)
    modes = jnp.concatenate([own_ref[...], recv_ref[...], shift_ref[...]], axis=0)
    v = dot(kron_ref[...], plane) + dot(modes, back_ref[0], ((0,), (0,)))
    a = math.sqrt(2.0 / math.pi)
    inner = v * (a + (a * 0.044715) * (v * v))
    half = 0.5 * v
    out_ref[...] = (half + half * jnp.tanh(inner)).astype(BF).reshape(C, 1, ROWS, DEPTH)


def shards(field, spectral_weight, point_weight, bias):
    front, along, back, planes = (jnp.asarray(t) for t in tables())
    chip = lax.axis_index("x")
    core = lax.axis_index("c")
    rows_at = (lax.axis_index("z") * DY + lax.axis_index("y")) * DC + core
    at = jnp.stack([core, chip, rows_at]).astype(jnp.int32)
    swap = [(0, 1), (1, 0)]
    bf = lambda *shape: jax.ShapeDtypeStruct(shape, BF)
    full = lambda *shape: pl.BlockSpec(shape, lambda *_: (0,) * len(shape))

    peer_weight = lax.ppermute(spectral_weight, "c", swap)

    own, send = pl.pallas_call(
        analysis_kernel,
        out_shape=(bf(128, 512), bf(128, 512)),
        grid_spec=pltpu.PrefetchScalarGridSpec(
            num_scalar_prefetch=1,
            grid=(X,),
            in_specs=[
                pl.BlockSpec((C, 1, ROWS, DEPTH), lambda x, at: (0, x, 0, 0)),
                pl.BlockSpec((1, 1, 1, 128, DEPTH), lambda x, at: (at[1], x, at[0], 0, 0)),
                pl.BlockSpec((1, 1, 1, 128, DEPTH), lambda x, at: (at[1], x, 1 - at[0], 0, 0)),
            ],
            out_specs=[full(128, 512), full(128, 512)],
            scratch_shapes=[pltpu.VMEM((128, 512), F32)] * 2,
        ),
        name="analysis",
    )(at, field, front, front)

    wy, kron, shift, spread = pl.pallas_call(
        tables_kernel,
        out_shape=(bf(512, 512), bf(512, 512), bf(16, 512), bf(256, 1024)),
        grid_spec=pltpu.PrefetchScalarGridSpec(
            num_scalar_prefetch=1,
            grid=(1,),
            in_specs=[
                pl.BlockSpec((1, 32, 32), lambda _, at: (at[2], 0, 0)),
                full(32, 32),
                full(1, 32),
            ],
            out_specs=[full(512, 512), full(512, 512), full(16, 512), full(256, 1024)],
        ),
        name="tables",
    )(at, along, point_weight, bias.reshape(1, 32))

    recv = lax.ppermute(send, "c", swap)
    parts = pl.pallas_call(
        rows_kernel,
        out_shape=bf(1024, 128),
        scratch_shapes=[pltpu.VMEM((1024, 128), F32)],
        name="rows",
    )(own, recv, wy)
    parts = lax.all_to_all(parts.reshape(128, 8, 128), ("x", "y", "z"), 0, 0, tiled=True)

    mixed = pl.pallas_call(
        mix_kernel,
        out_shape=bf(1024, 128),
        grid_spec=pltpu.PrefetchScalarGridSpec(
            num_scalar_prefetch=1,
            grid=(1,),
            in_specs=[full(1024, 128), full(4, 8, 1024), full(4, 8, 1024), full(256, 1024)],
            out_specs=full(1024, 128),
        ),
        name="mix",
    )(at, parts.reshape(1024, 128), spectral_weight, peer_weight, spread)
    modes = lax.all_to_all(mixed.reshape(128, 8, 128), ("x", "y", "z"), 0, 0, tiled=True)

    own, send = pl.pallas_call(
        modes_kernel,
        out_shape=(bf(128, 512), bf(128, 512)),
        scratch_shapes=[pltpu.VMEM((1024, 128), F32)],
        name="modes",
    )(modes.reshape(1024, 128), wy, planes)
    recv = lax.ppermute(send, "c", swap)

    return pl.pallas_call(
        grid_kernel,
        out_shape=bf(C, X, ROWS, DEPTH),
        grid_spec=pltpu.PrefetchScalarGridSpec(
            num_scalar_prefetch=1,
            grid=(X,),
            in_specs=[
                pl.BlockSpec((C, 1, ROWS, DEPTH), lambda x, at: (0, x, 0, 0)),
                full(512, 512),
                pl.BlockSpec((16, 512), lambda x, at: (x, 0)),
                pl.BlockSpec((16, 512), lambda x, at: (x, 0)),
                full(16, 512),
                pl.BlockSpec((1, 48, DEPTH), lambda x, at: (at[1] * 2 + at[0], 0, 0)),
            ],
            out_specs=pl.BlockSpec((C, 1, ROWS, DEPTH), lambda x, at: (0, x, 0, 0)),
        ),
        name="grid",
    )(at, field, kron, own, recv, shift, back)


def solution(mesh):
    fine = Mesh(mesh.devices.reshape(DZ, DY, DC, DX), ("z", "y", "c", "x"))
    return jax.shard_map(
        shards,
        mesh=fine,
        in_specs=(P(None, None, ("z", "y", "c"), "x"), P(("z", "y", "c"), "x", None), P(), P()),
        out_specs=P(None, None, ("z", "y", "c"), "x"),
        check_vma=False,
    )
```

time: 281 us -> 85.7 us (0.30)
  waiting for transfers between devices: 137 us -> 15.1 us
  blocking collectives: 84.4 us -> 19.9 us
  matrix products: 32.4 us -> 0 us
  Pallas kernels: 0 us -> 26.6 us
  starting transfers between devices: 0.01 us -> 20.7 us
  between operations: 14.2 us -> 0.03 us
  local copies, waits for them, and re-layouts: 12.5 us -> 2.01 us
    reduce_scatter x1 -> x0, waiting for transfers between devices: 137 us -> none  [shards(): lax.psum_scatter(partial_value, 'gy', scatter_dimension=1, tiled=True)]
    all_gather x2 -> x0, blocking collectives: 70.7 us -> none  [the longest x1 61.5 us: shards(): full_modes = lax.all_gather(widened, 'gy', axis=1, tiled=True)]
    dot_general x8 -> x0, matrix products: 32.4 us -> none  [the longest x1 7.72 us: shards(): spatial = jnp.einsum('cxyk,kz->cxyz', spatial, synth_z, precision=highest)]
    pallas_call x0 -> x6, Pallas kernels: none -> 26.6 us  [the longest x1 8.17 us: shards(): pl.pallas_call(grid_kernel, out_shape=bf(C, X, ROWS, DEPTH), grid_spec=pl...]
    all_to_all x0 -> x1, blocking collectives: none -> 19.9 us  [shards(): lax.all_to_all(mixed.reshape(128, 8, 128), ('x', 'y', 'z'), 0, 0, tiled=T...]
    all_to_all x0 -> x1, starting transfers between devices: none -> 13.8 us  [shards(): lax.all_to_all(parts.reshape(128, 8, 128), ('x', 'y', 'z'), 0, 0, tiled=T...]
    unnamed x1 -> x0, blocking collectives: 13.7 us -> none
    all_to_all x0 -> x1, waiting for transfers between devices: none -> 13 us  [shards(): lax.all_to_all(parts.reshape(128, 8, 128), ('x', 'y', 'z'), 0, 0, tiled=T...]
  transfers between devices with their start and end apart: 1 -> 4, of which waited for: 1 -> 3; matrix products, arithmetic and copies ran while one was open for 1% -> 0% of each run, Pallas kernels for 0% -> 4%
where the time goes in v1:
time: 85.7 us; the launch traced here: 85.1 us
  Pallas kernels  26.6 us (31%)
  starting transfers between devices  20.7 us (24%)
  blocking collectives  19.9 us (23%)
  waiting for transfers between devices  15.1 us (18%)
  local copies, waits for them, and re-layouts  2.01 us (2%)
    all_to_all x1, blocking collectives, shards(): lax.all_to_all(mixed.reshape(128, 8, 128), ('x', 'y', 'z'), 0, 0, tiled=T...  19.9 us
    all_to_all x1, starting transfers between devices, shards(): lax.all_to_all(parts.reshape(128, 8, 128), ('x', 'y', 'z'), 0, 0, tiled=T...  13.8 us
    all_to_all x1, waiting for transfers between devices, shards(): lax.all_to_all(parts.reshape(128, 8, 128), ('x', 'y', 'z'), 0, 0, tiled=T...  13 us
    pallas_call x1, Pallas kernels, shards(): pl.pallas_call(grid_kernel, out_shape=bf(C, X, ROWS, DEPTH), grid_spec=pl...  8.17 us
    pallas_call x1, Pallas kernels, shards(): pl.pallas_call(analysis_kernel, out_shape=(bf(128, 512), bf(128, 512)), g...  7.21 us
    ppermute x2, starting transfers between devices, shards(): recv = lax.ppermute(send, 'c', swap)  6.43 us
    pallas_call x1, Pallas kernels, shards(): pl.pallas_call(mix_kernel, out_shape=bf(1024, 128), grid_spec=pltpu.Prefe...  3.4 us
    pallas_call x1, Pallas kernels, shards(): pl.pallas_call(tables_kernel, out_shape=(bf(512, 512), bf(512, 512), bf(1...  2.98 us
  transfers between devices with their start and end apart: 4, of which 3 were waited for; matrix products, arithmetic and copies ran while one was open for 0% of the time, Pallas kernels for 4%

profile of v1, /device:TPU:1, one launch (start us, length us, event | category | flops | bytes accessed | tf_op | source)
XLA Modules:
  0.0 85.1 jit_solution(6070682916911384333)
XLA Ops:
  0.0 0.7 pad_add_fusion.at_ref
  0.7 7.2 %analysis.1 = (bf16[128,512]{1,0:T(8,128)(2,1)}, bf16[128,512]{1,0:T(8,128)(2,1)}) custom-call(s32[3]{0:T(128)} %pad_add_fusion.at_ref, bf16[32,8,16,256]{3,2,1,0:T(8,128)(2,1)} %field_ref.3, bf16[4,8,2,128,256]{4,3,2,1,0:T(8,128)(2,1)} %constant.29.clone.mine_ref.other_ref, bf16[4,8,2,128,256]{4,3,2,1,0:T(8,128)(2,1)} %constant.29.clone.mine_ref.other_ref), custom_call_target="tpu_custom_call" | custom-call | tf_op jit(solution)/shard_map/analysis/pallas_call | solution.py:222
  7.9 0.0 copy-start.3
  7.9 3.2 %collective-permute-start = (bf16[128,512]{1,0:T(8,128)(2,1)}, bf16[128,512]{1,0:T(8,128)(2,1)S(1)}, u32[]{:S(2)}, u32[]{:S(2)}) collective-permute-start(bf16[128,512]{1,0:T(8,128)(2,1)} %get-tuple-element.15), channel_id=1, source_target_pairs={{0,4},{4,0},{1,5},{5,1},{2,6},{6,2},{3,7},{7,3},{8,12},{12,8},{9,1... | collective-permute-start | bytes 393224 | tf_op jit(solution)/shard_map/ppermute | solution.py:255
  11.1 3.0 %tables.1 = (bf16[512,512]{1,0:T(8,128)(2,1)}, bf16[512,512]{1,0:T(8,128)(2,1)}, bf16[16,512]{1,0:T(8,128)(2,1)}, bf16[256,1024]{1,0:T(8,128)(2,1)}) custom-call(s32[3]{0:T(128)} %pad_add_fusion.at_ref, bf16[64,32,32]{2,1,0:T(8,128)(2,1)} %constant.30.clone.along_ref, bf16[32,32]{1,0:T(8,128)(2,1)} %point_ref.1, f32[1,32]{1,0:T(1,128)} %bitcast.12), custom_call_target="tpu_custom_call" | custom-call | tf_op jit(solution)/shard_map/tables/pallas_call | solution.py:239
  14.1 0.0 collective-permute-done.recv_ref
  14.1 0.0 copy-start.2
  14.1 0.7 copy-done.2
  14.8 2.3 %rows.1 = bf16[1024,128]{1,0:T(8,128)(2,1)} custom-call(bf16[128,512]{1,0:T(8,128)(2,1)} %get-tuple-element.14.own_ref, bf16[128,512]{1,0:T(8,128)(2,1)} %copy-done.2, bf16[512,512]{1,0:T(8,128)(2,1)} %get-tuple-element.16.wy_ref), custom_call_target="tpu_custom_call" | custom-call | tf_op jit(solution)/shard_map/rows/pallas_call | solution.py:256
  17.0 13.8 %all-to-all-start = ((bf16[128,8,128]{2,1,0:T(8,128)(2,1)}), bf16[128,8,128]{2,1,0:T(8,128)(2,1)S(1)}, u32[]{:S(2)}, u32[]{:S(2)}) async-start(bf16[128,8,128]{2,1,0:T(8,128)(2,1)} %bitcast.10), calls=%async_computation | async-start | bytes 524288 | tf_op jit(solution)/shard_map/all_to_all | solution.py:262
  30.8 0.0 copy-done.3
  30.8 0.5 collective-permute-start.1
  31.3 0.9 %collective-permute-done.1.peer_ref = bf16[4,8,1024]{2,1,0:T(8,128)(2,1)S(1)} collective-permute-done((bf16[4,8,1024]{2,1,0:T(8,128)(2,1)S(1)}, bf16[4,8,1024]{2,1,0:T(8,128)(2,1)S(1)}, u32[]{:S(2)}, u32[]{:S(2)}) %collective-permute-start.1) | collective-permute-done | bytes 65568 | tf_op jit(solution)/shard_map/ppermute | solution.py:220
  32.2 0.0 copy-start.4
  32.2 13.0 %all-to-all-done = bf16[128,8,128]{2,1,0:T(8,128)(2,1)S(1)} async-done(((bf16[128,8,128]{2,1,0:T(8,128)(2,1)}), bf16[128,8,128]{2,1,0:T(8,128)(2,1)S(1)}, u32[]{:S(2)}, u32[]{:S(2)}) %all-to-all-start) | async-done | bytes 262176 | tf_op jit(solution)/shard_map/all_to_all | solution.py:262
  45.2 0.0 copy-start
  45.2 0.0 copy-done.4
  45.2 0.7 copy-done
  45.9 3.4 %mix.1 = bf16[1024,128]{1,0:T(8,128)(2,1)} custom-call(s32[3]{0:T(128)} %pad_add_fusion.at_ref, bf16[1024,128]{1,0:T(8,128)(2,1)} %bitcast.9, bf16[4,8,1024]{2,1,0:T(8,128)(2,1)} %weight_ref.1, bf16[4,8,1024]{2,1,0:T(8,128)(2,1)} %copy-done.4, bf16[256,1024]{1,0:T(8,128)(2,1)} %get-tuple-element.17.spread_ref), custom_call_target="tpu_custom_call" | custom-call | tf_op jit(solution)/shard_map/mix/pallas_call | solution.py:264
  49.3 19.9 %all_to_all.10 = bf16[128,8,128]{2,1,0:T(8,128)(2,1)} all-to-all(bf16[128,8,128]{2,1,0:T(8,128)(2,1)} %bitcast.11), channel_id=1, replica_groups=mesh['z'=8,'y'=4,'c'=2,'x'=4] {'x','y','z'}, dimensions={0} | all-to-all | bytes 524288 | tf_op jit(solution)/shard_map/all_to_all | solution.py:275
  69.2 2.6 %modes.1 = (bf16[128,512]{1,0:T(8,128)(2,1)}, bf16[128,512]{1,0:T(8,128)(2,1)}) custom-call(bf16[1024,128]{1,0:T(8,128)(2,1)} %bitcast.8, bf16[512,512]{1,0:T(8,128)(2,1)} %get-tuple-element.16.wy_ref, bf16[128,128]{1,0:T(8,128)(2,1)} %constant.32.clone.planes_ref), custom_call_target="tpu_custom_call" | custom-call | tf_op jit(solution)/shard_map/modes/pallas_call | solution.py:277
  71.8 3.2 %collective-permute-start.2 = (bf16[128,512]{1,0:T(8,128)(2,1)}, bf16[128,512]{1,0:T(8,128)(2,1)S(1)}, u32[]{:S(2)}, u32[]{:S(2)}) collective-permute-start(bf16[128,512]{1,0:T(8,128)(2,1)} %get-tuple-element.19), channel_id=1, source_target_pairs={{0,4},{4,0},{1,5},{5,1},{2,6},{6,2},{3,7},{7,3},{8,12},{12,8},{9,1... | collective-permute-start | bytes 393224 | tf_op jit(solution)/shard_map/ppermute | solution.py:283
  75.0 1.2 %collective-permute-done.2.recv_ref = bf16[128,512]{1,0:T(8,128)(2,1)S(1)} collective-permute-done((bf16[128,512]{1,0:T(8,128)(2,1)}, bf16[128,512]{1,0:T(8,128)(2,1)S(1)}, u32[]{:S(2)}, u32[]{:S(2)}) %collective-permute-start.2) | collective-permute-done | bytes 131104 | tf_op jit(solution)/shard_map/ppermute | solution.py:283
  76.2 0.0 copy-start.1
  76.2 0.6 copy-done.1
  76.9 8.2 %grid.1 = bf16[32,8,16,256]{3,2,1,0:T(8,128)(2,1)} custom-call(s32[3]{0:T(128)} %pad_add_fusion.at_ref, bf16[32,8,16,256]{3,2,1,0:T(8,128)(2,1)} %field_ref.3, bf16[512,512]{1,0:T(8,128)(2,1)} %get-tuple-element.13.kron_ref, bf16[128,512]{1,0:T(8,128)(2,1)} %get-tuple-element.18.own_ref, bf16[128,512]{1,0:T(8,128)(2,1)} %copy-done.1, ...), custom_call_target="tpu_custom_call" | custom-call | tf_op jit(solution)/shard_map/grid/pallas_call | solution.py:285
Async XLA Ops:
  7.9 22.9 %copy-start.3 = (bf16[4,8,1024]{2,1,0:T(8,128)(2,1)S(1)}, bf16[4,8,1024]{2,1,0:T(8,128)(2,1)}, u32[]{:S(2)}) copy-start(bf16[4,8,1024]{2,1,0:T(8,128)(2,1)} %weight_ref.1) | copy-start | bytes 196612
  7.9 6.2 %collective-permute-start = (bf16[128,512]{1,0:T(8,128)(2,1)}, bf16[128,512]{1,0:T(8,128)(2,1)S(1)}, u32[]{:S(2)}, u32[]{:S(2)}) collective-permute-start(bf16[128,512]{1,0:T(8,128)(2,1)} %get-tuple-element.15), channel_id=1, source_target_pairs={{0,4},{4,0},{1,5},{5,1},{2,6},{6,2},{3,7},{7,3},{8,12},{12,8},{9,1... | collective-permute-start | bytes 393224 | tf_op jit(solution)/shard_map/ppermute | solution.py:255
  14.1 0.7 copy-start.2
  17.0 28.2 %all-to-all-start = ((bf16[128,8,128]{2,1,0:T(8,128)(2,1)}), bf16[128,8,128]{2,1,0:T(8,128)(2,1)S(1)}, u32[]{:S(2)}, u32[]{:S(2)}) async-start(bf16[128,8,128]{2,1,0:T(8,128)(2,1)} %bitcast.10), calls=%async_computation | async-start | bytes 524288 | tf_op jit(solution)/shard_map/all_to_all | solution.py:262
  30.8 1.4 %collective-permute-start.1 = (bf16[4,8,1024]{2,1,0:T(8,128)(2,1)S(1)}, bf16[4,8,1024]{2,1,0:T(8,128)(2,1)S(1)}, u32[]{:S(2)}, u32[]{:S(2)}) collective-permute-start(bf16[4,8,1024]{2,1,0:T(8,128)(2,1)S(1)} %copy-done.3), channel_id=1, source_target_pairs={{0,4},{4,0},{1,5},{5,1},{2,6},{6,2},{3,7},{7,3},{8,12},{12,8},{9,1... | collective-permute-start | bytes 196616 | tf_op jit(solution)/shard_map/ppermute | solution.py:220
  32.2 13.0 %copy-start.4 = (bf16[4,8,1024]{2,1,0:T(8,128)(2,1)}, bf16[4,8,1024]{2,1,0:T(8,128)(2,1)S(1)}, u32[]{:S(2)}) copy-start(bf16[4,8,1024]{2,1,0:T(8,128)(2,1)S(1)} %collective-permute-done.1.peer_ref) | copy-start | bytes 196612
  45.2 0.7 copy-start
  71.8 4.4 %collective-permute-start.2 = (bf16[128,512]{1,0:T(8,128)(2,1)}, bf16[128,512]{1,0:T(8,128)(2,1)S(1)}, u32[]{:S(2)}, u32[]{:S(2)}) collective-permute-start(bf16[128,512]{1,0:T(8,128)(2,1)} %get-tuple-element.19), channel_id=1, source_target_pairs={{0,4},{4,0},{1,5},{5,1},{2,6},{6,2},{3,7},{7,3},{8,12},{12,8},{9,1... | collective-permute-start | bytes 393224 | tf_op jit(solution)/shard_map/ppermute | solution.py:283
  76.2 0.7 copy-start.1

commit v2 on v1

v2 whole, which is shorter than its diff:
```python
import math

import jax
import jax.numpy as jnp
import ml_dtypes
import numpy as np
from jax import lax
from jax.experimental import pallas as pl
from jax.experimental.pallas import tpu as pltpu
from jax.sharding import Mesh
from jax.sharding import PartitionSpec as P

C, X, K, N = 32, 8, 32, 1024
DZ, DY, DC, DX = 8, 4, 2, 4
ROWS = N // (DZ * DY * DC)
DEPTH = N // DX
CHUNKS = 4
BF = jnp.bfloat16
F32 = jnp.float32


def cosines(count, length, norm):
    modes = np.arange(count, dtype=np.float64)[:, None]
    spots = np.arange(length, dtype=np.float64)[None, :]
    value = norm * np.cos(np.pi * modes * (spots + 0.5) / length)
    value[0] *= math.sqrt(0.5)
    return value


def tables():
    ax = cosines(X, X, math.sqrt(2.0 / X))
    ay = cosines(K, N, math.sqrt(2.0 / N))
    az = cosines(K, N, math.sqrt(2.0 / N)).astype(ml_dtypes.bfloat16).astype(np.float64)
    sz = cosines(K, N, math.sqrt(2.0 / K))
    kq, kx, i = np.meshgrid(np.arange(4), np.arange(DX), np.arange(X), indexing="ij")
    front = np.zeros((DX, DC, DEPTH, 2, 128))
    for core in range(DC):
        for h in range(2):
            k = (kx * 8 + (core ^ h) * 4 + kq).reshape(-1)
            front[:, core, :, h] = az[k].reshape(128, DX, DEPTH).transpose(1, 2, 0)
    across = np.tile(ax[i.reshape(-1)].T, (1, 2))
    along = np.zeros((DZ * DY * DC, 32, 32))
    for dev in range(DZ * DY * DC):
        core = dev % 2
        spots = np.concatenate([dev * ROWS + np.arange(ROWS), (dev ^ 1) * ROWS + np.arange(ROWS)])
        octet = np.concatenate([core * 4 + np.arange(4), (1 - core) * 4 + np.arange(4)])
        j = (np.arange(4)[:, None] * 8 + octet[None, :]).reshape(-1)
        along[dev] = ay[j][:, spots].T
    back = np.zeros((DX * DC, 48, DEPTH))
    q2, x2 = np.meshgrid(np.arange(4), np.arange(DX), indexing="ij")
    for chip in range(DX):
        for core in range(DC):
            own = (x2 * 8 + core * 4 + q2).reshape(-1)
            other = (x2 * 8 + (1 - core) * 4 + q2).reshape(-1)
            part = slice(chip * DEPTH, (chip + 1) * DEPTH)
            back[chip * 2 + core, :16] = sz[own][:, part]
            back[chip * 2 + core, 16:32] = sz[other][:, part]
            back[chip * 2 + core, 32:35] = 1.0
    planes = np.zeros((X, 16, 16, X))
    for m in range(16):
        planes[:, m, m, :] = ax.T * math.sqrt(N / K)
    bf = ml_dtypes.bfloat16
    return (
        front.reshape(DX, DC, DEPTH, 256).astype(bf),
        across.astype(np.float32),
        along.astype(bf),
        back.astype(bf),
        planes.reshape(128, 128).astype(bf),
    )


def dot(a, b, dims=((1,), (0,))):
    return lax.dot_general(a, b, (dims, ((), ())), preferred_element_type=F32)


def iota(shape, dim):
    return lax.broadcasted_iota(jnp.int32, shape, dim)


def ones_where(condition):
    return jnp.where(condition, 1.0, 0.0).astype(BF)


def at_chip():
    return lax.axis_index("x")


def at_core():
    return lax.axis_index("c")


def at_rows():
    return (lax.axis_index("z") * DY + lax.axis_index("y")) * DC + lax.axis_index("c")


def analysis_kernel(
    field, front, across, along, own, send, wy, grid, weights, base, vectors, piece, field_sem, sems
):
    loads = [
        pltpu.make_async_copy(front.at[at_chip(), at_core()], base, sems.at[0]),
        pltpu.make_async_copy(across, vectors, sems.at[1]),
        pltpu.make_async_copy(along.at[at_rows()], piece, sems.at[2]),
    ]
    for load in loads:
        load.start()
    copy = pltpu.make_async_copy(field, grid, field_sem)
    copy.start()
    for load in loads:
        load.wait()
    wide = base[...].astype(F32)
    for x in range(X):
        weights[pl.ds(x * DEPTH, DEPTH), :] = (wide * vectors[pl.ds(x, 1), :]).astype(BF)
    p1 = ones_where(
        (iota((512, 32), 0) // 256 == iota((512, 32), 1) // 16)
        & (iota((512, 32), 0) % 16 == iota((512, 32), 1) % 16)
    )
    p2 = ones_where(
        (iota((32, 512), 0) // 8 == iota((32, 512), 1) // 128)
        & (iota((32, 512), 0) % 8 == iota((32, 512), 1) % 8)
    )
    same = (iota((512, 512), 0) // 16) % 16 == (iota((512, 512), 1) // 8) % 16
    full = dot(dot(p1, piece[...]).astype(BF), p2)
    wy[...] = jnp.where(same, full, 0.0).astype(BF)
    copy.wait()
    lhs = jnp.concatenate([grid[:, x].reshape(C * ROWS, DEPTH) for x in range(X)], axis=1)
    res = dot(lhs, weights[...]).T.astype(BF)
    own[...] = res[:128]
    send[...] = res[128:]


def tables_kernel(
    point_ref, bias_ref, back_ref, planes_ref, after_ref, kron_ref, shift_ref, spread_ref, back_out, planes_out, sems
):
    loads = [
        pltpu.make_async_copy(back_ref.at[at_chip() * DC + at_core()], back_out, sems.at[0]),
        pltpu.make_async_copy(planes_ref, planes_out, sems.at[1]),
    ]
    for load in loads:
        load.start()
    e1 = ones_where(iota((512, 32), 0) // 16 == iota((512, 32), 1))
    e2 = ones_where(iota((32, 512), 0) == iota((32, 512), 1) // 16)
    wide = dot(dot(e1, point_ref[...], ((1,), (1,))).astype(BF), e2)
    same = iota((512, 512), 0) % 16 == iota((512, 512), 1) % 16
    kron_ref[...] = jnp.where(same, wide, 0.0).astype(BF)
    b = jnp.broadcast_to(bias_ref[...], (16, 32))
    b1 = b.astype(BF).astype(F32)
    b2 = (b - b1).astype(BF).astype(F32)
    b3 = b - b1 - b2
    row = iota((16, 32), 0)
    parts = jnp.where(row == 0, b1, jnp.where(row == 1, b2, jnp.where(row == 2, b3, 0.0)))
    shift_ref[...] = dot(parts.astype(BF), e2).astype(BF)
    spread_ref[...] = ones_where(iota((128, 512), 0) // 8 == iota((128, 512), 1) // 32)
    for load in loads:
        load.wait()


def rows_kernel(own_ref, recv_ref, wy_ref, out_ref, scratch):
    for g in range(2):
        half = pl.ds(g * 256, 256)
        lhs = jnp.concatenate([own_ref[:, half], recv_ref[:, half]], axis=1)
        res = dot(lhs, wy_ref[...])
        for kq in range(4):
            for kx in range(4):
                for joct in range(4):
                    start = (kx * 4 + joct) * 64 + g * 4 + kq
                    first = (kq * 4 + kx) * 8
                    scratch[pl.ds(start, 8, stride=8), :] = res[
                        first : first + 8, joct * 128 : (joct + 1) * 128
                    ]
    out_ref[...] = scratch[...].astype(BF)


def mix_kernel(parts_ref, weight_ref, peer_ref, spread_ref, out_ref):
    core = at_core()
    s = jnp.sum(parts_ref[...].astype(F32).reshape(128, 8, 128), axis=0)
    row = iota((8, 128), 0)
    turned = pltpu.roll(s, 4, 0)
    s8 = jnp.concatenate([jnp.where(row < 4, s, turned), jnp.where(row < 4, turned, s)], axis=1)
    s64 = jnp.concatenate([s8] * 8, axis=0)
    row = iota((64, 256), 0)
    keep = (iota((64, 256), 1) % 8 == row // 8) & ((row % 8) // 4 == core)
    s64 = jnp.where(keep, s64, 0.0)
    high = s64.astype(BF)
    low = (s64 - high.astype(F32)).astype(BF)
    spread = spread_ref[...]
    halves = [dot(high[:, part], spread) + dot(low[:, part], spread) for part in (slice(0, 128), slice(128, 256))]
    wide = jnp.concatenate(halves, axis=1)
    weight = jnp.concatenate(
        [weight_ref[...].astype(F32).reshape(32, 1024), peer_ref[...].astype(F32).reshape(32, 1024)], axis=0
    )
    prod = wide * weight
    total = prod[:, 0:128]
    for part in range(1, 8):
        total = total + prod[:, part * 128 : (part + 1) * 128]
    total = total + pltpu.roll(total, 64, 1)
    total = total + pltpu.roll(total, 32, 1)
    mixed = total.astype(BF)
    q, col = iota((128, 256), 0), iota((128, 256), 1)
    place = ones_where(q == (col // 128) * 16 + (col % 128) // 8)
    placed = dot(mixed, place)
    placed = jnp.where(iota((64, 256), 1) % 8 == iota((64, 256), 0) // 8, placed, 0.0).astype(BF)
    take = ones_where(iota((8, 64), 0) % 4 == iota((8, 64), 1) % 4)
    both = dot(take, placed)
    out = jnp.where(iota((8, 128), 0) < 4, both[:, :128], both[:, 128:])
    out_ref[...] = jnp.broadcast_to(out[None], (128, 8, 128)).reshape(1024, 128).astype(BF)


def modes_kernel(modes_ref, wy_ref, planes_ref, after_ref, own_ref, send_ref, scratch):
    scratch[...] = modes_ref[...].astype(F32)
    for g in range(2):
        cols = []
        for joct in range(4):
            pieces = []
            for kq in range(4):
                for kx in range(4):
                    start = (kx * 4 + joct) * 64 + g * 4 + kq
                    pieces.append(scratch[pl.ds(start, 8, stride=8), :])
            cols.append(jnp.concatenate(pieces, axis=0))
        lhs = jnp.concatenate(cols, axis=1).astype(BF)
        res = dot(lhs, wy_ref[...], ((1,), (1,))).astype(BF)
        res = dot(planes_ref[...], res).astype(BF)
        half = pl.ds(g * 256, 256)
        own_ref[:, half] = res[:, :256]
        send_ref[:, half] = res[:, 256:]


def point_kernel(field, kron_ref, after_ref, out_ref, grid, sem):
    copy = pltpu.make_async_copy(field, grid, sem)
    copy.start()
    copy.wait()
    for x in range(X):
        out_ref[x] = dot(kron_ref[...], grid[:, x].reshape(C * ROWS, DEPTH)).astype(BF)


def grid_kernel(point_ref, own_ref, recv_ref, shift_ref, back_ref, out_ref, stage, sems):
    a = 2.0 * math.sqrt(2.0 / math.pi)
    share = C // CHUNKS
    copies = []
    for q in range(CHUNKS):
        cols = pl.ds(q * share * ROWS, share * ROWS)
        rows = pl.ds(q * share, share)
        for x in range(X):
            part = pl.ds(x * 16, 16)
            modes = jnp.concatenate([own_ref[part, cols], recv_ref[part, cols], shift_ref[:, cols]], axis=0)
            v = point_ref[x, cols, :].astype(F32) + dot(modes, back_ref[...], ((0,), (0,)))
            v = v * jax.nn.sigmoid(v * (a + (a * 0.044715) * (v * v)))
            stage[rows, x] = v.astype(BF).reshape(share, ROWS, DEPTH)
        copies.append(pltpu.make_async_copy(stage.at[rows], out_ref.at[rows], sems.at[q]))
        copies[-1].start()
    for copy in copies:
        copy.wait()


def call(kernel, name, args, outs, scratch=(), spaces=None):
    spaces = spaces or [pltpu.VMEM] * len(args)
    args = [x if s is pl.ANY else pltpu.with_memory_space_constraint(x, s) for x, s in zip(args, spaces)]
    spec = lambda s: pl.BlockSpec(memory_space=pl.ANY if s is pltpu.HBM else s)
    return pl.pallas_call(
        kernel,
        out_shape=outs,
        in_specs=[spec(s) for s in spaces],
        out_specs=jax.tree.map(lambda o: spec(o.memory_space), outs),
        scratch_shapes=list(scratch),
        compiler_params=pltpu.CompilerParams(vmem_limit_bytes=12 * 2**20),
        name=name,
    )(*args)


def shards(field, spectral_weight, point_weight, bias):
    front, across, along, back, planes = (jnp.asarray(t) for t in tables())
    swap = [(0, 1), (1, 0)]
    vm = lambda *shape, dtype=BF: pltpu.VMEM(shape, dtype)
    dma = pltpu.SemaphoreType.DMA

    peer_weight = lax.ppermute(spectral_weight, "c", swap)
    own, send, wy = call(
        analysis_kernel,
        "analysis",
        (field, front, across, along),
        (vm(128, 512), vm(128, 512), vm(512, 512)),
        (
            vm(C, X, ROWS, DEPTH),
            vm(X * DEPTH, 256),
            vm(DEPTH, 256),
            vm(X, 256, dtype=F32),
            vm(32, 32),
            dma,
            dma((3,)),
        ),
        (pltpu.HBM,) * 4,
    )
    recv = lax.ppermute(send, "c", swap)
    parts = call(rows_kernel, "rows", (own, recv, wy), vm(1024, 128), (vm(1024, 128, dtype=F32),))
    kron, shift, spread, back, planes = call(
        tables_kernel,
        "tables",
        (point_weight, bias.reshape(1, 32), back, planes, parts),
        (vm(512, 512), vm(16, 512), vm(128, 512), vm(48, DEPTH), vm(128, 128)),
        (dma((2,)),),
        (pltpu.VMEM, pltpu.VMEM, pltpu.HBM, pltpu.HBM, pl.ANY),
    )
    parts = lax.all_to_all(parts.reshape(128, 8, 128), ("x", "y", "z"), 0, 0, tiled=True)
    mixed = call(
        mix_kernel,
        "mix",
        (parts.reshape(1024, 128), spectral_weight, peer_weight, spread),
        vm(1024, 128),
    )
    point = call(
        point_kernel,
        "point",
        (field, kron, mixed),
        vm(X, C * ROWS, DEPTH),
        (vm(C, X, ROWS, DEPTH), dma),
        (pltpu.HBM, pltpu.VMEM, pl.ANY),
    )
    modes = lax.all_to_all(mixed.reshape(128, 8, 128), ("x", "y", "z"), 0, 0, tiled=True)
    own, send = call(
        modes_kernel,
        "modes",
        (modes.reshape(1024, 128), wy, planes, point),
        (vm(128, 512), vm(128, 512)),
        (vm(1024, 128, dtype=F32),),
        (pltpu.VMEM, pltpu.VMEM, pltpu.VMEM, pl.ANY),
    )
    recv = lax.ppermute(send, "c", swap)
    return call(
        grid_kernel,
        "grid",
        (point, own, recv, shift, back),
        pltpu.HBM((C, X, ROWS, DEPTH), BF),
        (vm(C, X, ROWS, DEPTH), dma((CHUNKS,))),
    )


def solution(mesh):
    fine = Mesh(mesh.devices.reshape(DZ, DY, DC, DX), ("z", "y", "c", "x"))
    return jax.shard_map(
        shards,
        mesh=fine,
        in_specs=(P(None, None, ("z", "y", "c"), "x"), P(("z", "y", "c"), "x", None), P(), P()),
        out_specs=P(None, None, ("z", "y", "c"), "x"),
        check_vma=False,
    )
```

time: 85.7 us -> 64.6 us (0.75)
  blocking collectives: 19.9 us -> 0 us
  Pallas kernels: 26.6 us -> 12.5 us
  waiting for transfers between devices: 15.1 us -> 24.2 us
  starting transfers between devices: 20.7 us -> 27.4 us
  local copies, waits for them, and re-layouts: 2.01 us -> 0.01 us
    all_to_all x1 -> x0, blocking collectives: 19.9 us -> none  [shards(): lax.all_to_all(mixed.reshape(128, 8, 128), ('x', 'y', 'z'), 0, 0, tiled=T...]
    pallas_call x6 -> x7, Pallas kernels: 26.6 us -> 12.5 us  [call(): pl.pallas_call(kernel, out_shape=outs, in_specs=[spec(s) for s in spaces]...]
    all_to_all x0 -> x1, waiting for transfers between devices: none -> 9.96 us  [shards(): lax.all_to_all(mixed.reshape(128, 8, 128), ('x', 'y', 'z'), 0, 0, tiled=T...]
    all_to_all x0 -> x1, starting transfers between devices: none -> 6.29 us  [shards(): lax.all_to_all(mixed.reshape(128, 8, 128), ('x', 'y', 'z'), 0, 0, tiled=T...]
    unnamed x10 -> x6, local copies, waits for them, and re-layouts: 2.01 us -> 0.01 us
    ppermute x1, waiting for transfers between devices: 0.9 us -> 0.01 us  [shards(): peer_weight = lax.ppermute(spectral_weight, 'c', swap)]
  transfers between devices with their start and end apart: 4 -> 5, of which waited for: 3 -> 4; matrix products, arithmetic and copies ran while one was open for 0% -> 0% of each run, Pallas kernels for 4% -> 6%
where the time goes in v2:
time: 64.6 us; the launch traced here: 64.2 us
  starting transfers between devices  27.4 us (42%)
  waiting for transfers between devices  24.2 us (37%)
  Pallas kernels  12.5 us (19%)
    all_to_all x1, starting transfers between devices, shards(): lax.all_to_all(parts.reshape(128, 8, 128), ('x', 'y', 'z'), 0, 0, tiled=T...  13.8 us
    pallas_call x7, Pallas kernels, call(): pl.pallas_call(kernel, out_shape=outs, in_specs=[spec(s) for s in spaces]...  12.5 us
    all_to_all x1, waiting for transfers between devices, shards(): lax.all_to_all(parts.reshape(128, 8, 128), ('x', 'y', 'z'), 0, 0, tiled=T...  12.3 us
    all_to_all x1, waiting for transfers between devices, shards(): lax.all_to_all(mixed.reshape(128, 8, 128), ('x', 'y', 'z'), 0, 0, tiled=T...  9.96 us
    ppermute x2, starting transfers between devices, shards(): recv = lax.ppermute(send, 'c', swap)  6.59 us
    all_to_all x1, starting transfers between devices, shards(): lax.all_to_all(mixed.reshape(128, 8, 128), ('x', 'y', 'z'), 0, 0, tiled=T...  6.29 us
    ppermute x2, waiting for transfers between devices, shards(): recv = lax.ppermute(send, 'c', swap)  1.97 us
  transfers between devices with their start and end apart: 5, of which 4 were waited for; matrix products, arithmetic and copies ran while one was open for 0% of the time, Pallas kernels for 6%

profile of v2, /device:TPU:1, one launch (start us, length us, event | category | flops | bytes accessed | tf_op | source)
XLA Modules:
  0.0 64.2 jit_solution(16385262791084392536)
XLA Ops:
  0.0 0.0 copy-start
  0.0 0.0 copy-start.2
  0.0 0.0 copy-start.1
  0.0 3.0 %analysis.1 = (bf16[128,512]{1,0:T(8,128)(2,1)S(1)}, bf16[128,512]{1,0:T(8,128)(2,1)S(1)}, bf16[512,512]{1,0:T(8,128)(2,1)S(1)}) custom-call(bf16[32,8,16,256]{3,2,1,0:T(8,128)(2,1)} %field.3, bf16[4,2,256,256]{3,2,1,0:T(8,128)(2,1)} %constant.10.clone.front, f32[8,256]{1,0:T(8,128)} %constant.11.clone.across, bf16[64,32,32]{2,1,0:T(8,128)(2,1)} %constant.12.clone.along), custom_call_target="tpu_custom_call" | custom-call | tf_op jit(solution)/shard_map/analysis/pallas_call | solution.py:258
  3.1 3.3 %collective-permute-start = (bf16[128,512]{1,0:T(8,128)(2,1)S(1)}, bf16[128,512]{1,0:T(8,128)(2,1)S(1)}, u32[]{:S(2)}, u32[]{:S(2)}) collective-permute-start(bf16[128,512]{1,0:T(8,128)(2,1)S(1)} %get-tuple-element.16), channel_id=1, source_target_pairs={{0,4},{4,0},{1,5},{5,1},{2,6},{6,2},{3,7},{7,3},{8,12},{12,8},{9,1... | collective-permute-start | bytes 393224 | tf_op jit(solution)/shard_map/ppermute | solution.py:292
  6.4 1.0 %collective-permute-done.recv_ref = bf16[128,512]{1,0:T(8,128)(2,1)S(1)} collective-permute-done((bf16[128,512]{1,0:T(8,128)(2,1)S(1)}, bf16[128,512]{1,0:T(8,128)(2,1)S(1)}, u32[]{:S(2)}, u32[]{:S(2)}) %collective-permute-start) | collective-permute-done | bytes 131104 | tf_op jit(solution)/shard_map/ppermute | solution.py:292
  7.3 1.1 %rows.1.after_ref = bf16[1024,128]{1,0:T(8,128)(2,1)} custom-call(bf16[128,512]{1,0:T(8,128)(2,1)S(1)} %get-tuple-element.15.own_ref, bf16[128,512]{1,0:T(8,128)(2,1)S(1)} %collective-permute-done.recv_ref, bf16[512,512]{1,0:T(8,128)(2,1)S(1)} %get-tuple-element.17.wy_ref), custom_call_target="tpu_custom_call" | custom-call | tf_op jit(solution)/shard_map/rows/pallas_call | solution.py:258
  8.4 13.8 %all-to-all-start = ((bf16[128,8,128]{2,1,0:T(8,128)(2,1)}), bf16[128,8,128]{2,1,0:T(8,128)(2,1)S(1)}, u32[]{:S(2)}, u32[]{:S(2)}) async-start(bf16[128,8,128]{2,1,0:T(8,128)(2,1)} %bitcast.1), calls=%async_computation | async-start | bytes 524288 | tf_op jit(solution)/shard_map/all_to_all | solution.py:302
  22.2 0.0 copy-done
  22.2 0.7 %collective-permute-start.1 = (bf16[4,8,1024]{2,1,0:T(8,128)(2,1)S(1)}, bf16[4,8,1024]{2,1,0:T(8,128)(2,1)S(1)}, u32[]{:S(2)}, u32[]{:S(2)}) collective-permute-start(bf16[4,8,1024]{2,1,0:T(8,128)(2,1)S(1)} %copy-done), channel_id=1, source_target_pairs={{0,4},{4,0},{1,5},{5,1},{2,6},{6,2},{3,7},{7,3},{8,12},{12,8},{9,1... | collective-permute-start | bytes 196616 | tf_op jit(solution)/shard_map/ppermute | solution.py:275
  23.0 0.0 copy-done.2
  23.0 0.0 copy-done.1
  23.0 1.0 %tables.1 = (bf16[512,512]{1,0:T(8,128)(2,1)S(1)}, bf16[16,512]{1,0:T(8,128)(2,1)S(1)}, bf16[128,512]{1,0:T(8,128)(2,1)S(1)}, bf16[48,256]{1,0:T(8,128)(2,1)S(1)}, bf16[128,128]{1,0:T(8,128)(2,1)S(1)}) custom-call(bf16[32,32]{1,0:T(8,128)(2,1)S(1)} %copy-done.1, f32[1,32]{1,0:T(1,128)S(1)} %bitcast.7, bf16[8,48,256]{2,1,0:T(8,128)(2,1)} %constant.13.clone.back_ref, ...), custom_call_target="tpu_custom_call" | custom-call | tf_op jit(solution)/shard_map/tables/pallas_call | solution.py:258
  24.0 0.0 collective-permute-done.1.peer_ref
  24.0 12.3 %all-to-all-done = bf16[128,8,128]{2,1,0:T(8,128)(2,1)S(1)} async-done(((bf16[128,8,128]{2,1,0:T(8,128)(2,1)}), bf16[128,8,128]{2,1,0:T(8,128)(2,1)S(1)}, u32[]{:S(2)}, u32[]{:S(2)}) %all-to-all-start) | async-done | bytes 262176 | tf_op jit(solution)/shard_map/all_to_all | solution.py:302
  36.3 1.5 %mix.1.after_ref = bf16[1024,128]{1,0:T(8,128)(2,1)} custom-call(bf16[1024,128]{1,0:T(8,128)(2,1)S(1)} %bitcast.5, bf16[4,8,1024]{2,1,0:T(8,128)(2,1)S(1)} %copy-done, bf16[4,8,1024]{2,1,0:T(8,128)(2,1)S(1)} %collective-permute-done.1.peer_ref, bf16[128,512]{1,0:T(8,128)(2,1)S(1)} %get-tuple-element.19.spread_ref), custom_call_target="tpu_custom_call" | custom-call | tf_op jit(solution)/shard_map/mix/pallas_call | solution.py:258
  37.7 6.3 %all-to-all-start.1 = ((bf16[128,8,128]{2,1,0:T(8,128)(2,1)}), bf16[128,8,128]{2,1,0:T(8,128)(2,1)S(1)}, u32[]{:S(2)}, u32[]{:S(2)}) async-start(bf16[128,8,128]{2,1,0:T(8,128)(2,1)} %bitcast.3), calls=%async_computation.1 | async-start | bytes 524288 | tf_op jit(solution)/shard_map/all_to_all | solution.py:317
  44.0 2.9 %point.1.after_ref.point_ref = bf16[8,512,256]{2,1,0:T(8,128)(2,1)S(1)} custom-call(bf16[32,8,16,256]{3,2,1,0:T(8,128)(2,1)} %field.3, bf16[512,512]{1,0:T(8,128)(2,1)S(1)} %get-tuple-element.18.kron_ref, bf16[1024,128]{1,0:T(8,128)(2,1)} %mix.1.after_ref), custom_call_target="tpu_custom_call" | custom-call | tf_op jit(solution)/shard_map/point/pallas_call | solution.py:258
  46.9 10.0 %all-to-all-done.1 = bf16[128,8,128]{2,1,0:T(8,128)(2,1)S(1)} async-done(((bf16[128,8,128]{2,1,0:T(8,128)(2,1)}), bf16[128,8,128]{2,1,0:T(8,128)(2,1)S(1)}, u32[]{:S(2)}, u32[]{:S(2)}) %all-to-all-start.1) | async-done | bytes 262176 | tf_op jit(solution)/shard_map/all_to_all | solution.py:317
  56.8 0.8 %modes.1 = (bf16[128,512]{1,0:T(8,128)(2,1)S(1)}, bf16[128,512]{1,0:T(8,128)(2,1)S(1)}) custom-call(bf16[1024,128]{1,0:T(8,128)(2,1)S(1)} %bitcast.6, bf16[512,512]{1,0:T(8,128)(2,1)S(1)} %get-tuple-element.17.wy_ref, bf16[128,128]{1,0:T(8,128)(2,1)S(1)} %get-tuple-element.20.planes_ref, bf16[8,512,256]{2,1,0:T(8,128)(2,1)S(1)} %point.1.after_ref.point_ref), custom_call_target="tpu_custom_call" | custom-call | tf_op jit(solution)/shard_map/modes/pallas_call | solution.py:258
  57.6 3.3 %collective-permute-start.2 = (bf16[128,512]{1,0:T(8,128)(2,1)S(1)}, bf16[128,512]{1,0:T(8,128)(2,1)S(1)}, u32[]{:S(2)}, u32[]{:S(2)}) collective-permute-start(bf16[128,512]{1,0:T(8,128)(2,1)S(1)} %get-tuple-element.22), channel_id=1, source_target_pairs={{0,4},{4,0},{1,5},{5,1},{2,6},{6,2},{3,7},{7,3},{8,12},{12,8},{9,1... | collective-permute-start | bytes 393224 | tf_op jit(solution)/shard_map/ppermute | solution.py:326
  60.9 1.0 %collective-permute-done.2.recv_ref = bf16[128,512]{1,0:T(8,128)(2,1)S(1)} collective-permute-done((bf16[128,512]{1,0:T(8,128)(2,1)S(1)}, bf16[128,512]{1,0:T(8,128)(2,1)S(1)}, u32[]{:S(2)}, u32[]{:S(2)}) %collective-permute-start.2) | collective-permute-done | bytes 131104 | tf_op jit(solution)/shard_map/ppermute | solution.py:326
  61.9 2.3 %grid.1 = bf16[32,8,16,256]{3,2,1,0:T(8,128)(2,1)} custom-call(bf16[8,512,256]{2,1,0:T(8,128)(2,1)S(1)} %point.1.after_ref.point_ref, bf16[128,512]{1,0:T(8,128)(2,1)S(1)} %get-tuple-element.21.own_ref, bf16[128,512]{1,0:T(8,128)(2,1)S(1)} %collective-permute-done.2.recv_ref, bf16[16,512]{1,0:T(8,128)(2,1)S(1)} %get-tuple-element.23.shift_ref, ...), custom_call_target="tpu_custom_call" | custom-call | tf_op jit(solution)/shard_map/grid/pallas_call | solution.py:258
Async XLA Ops:
  0.0 22.2 %copy-start = (bf16[4,8,1024]{2,1,0:T(8,128)(2,1)S(1)}, bf16[4,8,1024]{2,1,0:T(8,128)(2,1)}, u32[]{:S(2)}) copy-start(bf16[4,8,1024]{2,1,0:T(8,128)(2,1)} %weight_ref.1) | copy-start | bytes 196612
  0.0 23.0 %copy-start.2 = (f32[32]{0:T(128)S(1)}, f32[32]{0:T(128)}, u32[]{:S(2)}) copy-start(f32[32]{0:T(128)} %param.12) | copy-start | bytes 388
  0.0 23.0 %copy-start.1 = (bf16[32,32]{1,0:T(8,128)(2,1)S(1)}, bf16[32,32]{1,0:T(8,128)(2,1)}, u32[]{:S(2)}) copy-start(bf16[32,32]{1,0:T(8,128)(2,1)} %point_ref.1) | copy-start | bytes 6148
  3.1 4.3 %collective-permute-start = (bf16[128,512]{1,0:T(8,128)(2,1)S(1)}, bf16[128,512]{1,0:T(8,128)(2,1)S(1)}, u32[]{:S(2)}, u32[]{:S(2)}) collective-permute-start(bf16[128,512]{1,0:T(8,128)(2,1)S(1)} %get-tuple-element.16), channel_id=1, source_target_pairs={{0,4},{4,0},{1,5},{5,1},{2,6},{6,2},{3,7},{7,3},{8,12},{12,8},{9,1... | collective-permute-start | bytes 393224 | tf_op jit(solution)/shard_map/ppermute | solution.py:292
  8.4 27.8 %all-to-all-start = ((bf16[128,8,128]{2,1,0:T(8,128)(2,1)}), bf16[128,8,128]{2,1,0:T(8,128)(2,1)S(1)}, u32[]{:S(2)}, u32[]{:S(2)}) async-start(bf16[128,8,128]{2,1,0:T(8,128)(2,1)} %bitcast.1), calls=%async_computation | async-start | bytes 524288 | tf_op jit(solution)/shard_map/all_to_all | solution.py:302
  22.2 1.7 %collective-permute-start.1 = (bf16[4,8,1024]{2,1,0:T(8,128)(2,1)S(1)}, bf16[4,8,1024]{2,1,0:T(8,128)(2,1)S(1)}, u32[]{:S(2)}, u32[]{:S(2)}) collective-permute-start(bf16[4,8,1024]{2,1,0:T(8,128)(2,1)S(1)} %copy-done), channel_id=1, source_target_pairs={{0,4},{4,0},{1,5},{5,1},{2,6},{6,2},{3,7},{7,3},{8,12},{12,8},{9,1... | collective-permute-start | bytes 196616 | tf_op jit(solution)/shard_map/ppermute | solution.py:275
  37.7 19.1 %all-to-all-start.1 = ((bf16[128,8,128]{2,1,0:T(8,128)(2,1)}), bf16[128,8,128]{2,1,0:T(8,128)(2,1)S(1)}, u32[]{:S(2)}, u32[]{:S(2)}) async-start(bf16[128,8,128]{2,1,0:T(8,128)(2,1)} %bitcast.3), calls=%async_computation.1 | async-start | bytes 524288 | tf_op jit(solution)/shard_map/all_to_all | solution.py:317
  57.6 4.3 %collective-permute-start.2 = (bf16[128,512]{1,0:T(8,128)(2,1)S(1)}, bf16[128,512]{1,0:T(8,128)(2,1)S(1)}, u32[]{:S(2)}, u32[]{:S(2)}) collective-permute-start(bf16[128,512]{1,0:T(8,128)(2,1)S(1)} %get-tuple-element.22), channel_id=1, source_target_pairs={{0,4},{4,0},{1,5},{5,1},{2,6},{6,2},{3,7},{7,3},{8,12},{12,8},{9,1... | collective-permute-start | bytes 393224 | tf_op jit(solution)/shard_map/ppermute | solution.py:326

commit v3 on v2

--- a/solution.py
+++ b/solution.py
@@ -94,49 +94,37 @@
 
 
 def analysis_kernel(
-    field, front, across, along, own, send, wy, grid, weights, base, vectors, piece, field_sem, sems
+    field, front, across, back, planes, own, send, back_out, planes_out, grid, weights, base, vectors, field_sem, sems
 ):
     loads = [
         pltpu.make_async_copy(front.at[at_chip(), at_core()], base, sems.at[0]),
         pltpu.make_async_copy(across, vectors, sems.at[1]),
-        pltpu.make_async_copy(along.at[at_rows()], piece, sems.at[2]),
+        pltpu.make_async_copy(back.at[at_chip() * DC + at_core()], back_out, sems.at[2]),
+        pltpu.make_async_copy(planes, planes_out, sems.at[3]),
     ]
-    for load in loads:
-        load.start()
     copy = pltpu.make_async_copy(field, grid, field_sem)
+    loads[0].start()
+    loads[1].start()
     copy.start()
-    for load in loads:
-        load.wait()
+    loads[2].start()
+    loads[3].start()
+    loads[0].wait()
+    loads[1].wait()
     wide = base[...].astype(F32)
     for x in range(X):
         weights[pl.ds(x * DEPTH, DEPTH), :] = (wide * vectors[pl.ds(x, 1), :]).astype(BF)
-    p1 = ones_where(
-        (iota((512, 32), 0) // 256 == iota((512, 32), 1) // 16)
-        & (iota((512, 32), 0) % 16 == iota((512, 32), 1) % 16)
-    )
-    p2 = ones_where(
-        (iota((32, 512), 0) // 8 == iota((32, 512), 1) // 128)
-        & (iota((32, 512), 0) % 8 == iota((32, 512), 1) % 8)
-    )
-    same = (iota((512, 512), 0) // 16) % 16 == (iota((512, 512), 1) // 8) % 16
-    full = dot(dot(p1, piece[...]).astype(BF), p2)
-    wy[...] = jnp.where(same, full, 0.0).astype(BF)
     copy.wait()
     lhs = jnp.concatenate([grid[:, x].reshape(C * ROWS, DEPTH) for x in range(X)], axis=1)
     res = dot(lhs, weights[...]).T.astype(BF)
     own[...] = res[:128]
     send[...] = res[128:]
-
-
-def tables_kernel(
-    point_ref, bias_ref, back_ref, planes_ref, after_ref, kron_ref, shift_ref, spread_ref, back_out, planes_out, sems
-):
-    loads = [
-        pltpu.make_async_copy(back_ref.at[at_chip() * DC + at_core()], back_out, sems.at[0]),
-        pltpu.make_async_copy(planes_ref, planes_out, sems.at[1]),
-    ]
-    for load in loads:
-        load.start()
+    loads[2].wait()
+    loads[3].wait()
+
+
+def tables_kernel(along, point_ref, bias_ref, wy, kron_ref, shift_ref, spread_ref, piece, sem):
+    load = pltpu.make_async_copy(along.at[at_rows()], piece, sem)
+    load.start()
     e1 = ones_where(iota((512, 32), 0) // 16 == iota((512, 32), 1))
     e2 = ones_where(iota((32, 512), 0) == iota((32, 512), 1) // 16)
     wide = dot(dot(e1, point_ref[...], ((1,), (1,))).astype(BF), e2)
@@ -150,23 +138,34 @@
     parts = jnp.where(row == 0, b1, jnp.where(row == 1, b2, jnp.where(row == 2, b3, 0.0)))
     shift_ref[...] = dot(parts.astype(BF), e2).astype(BF)
     spread_ref[...] = ones_where(iota((128, 512), 0) // 8 == iota((128, 512), 1) // 32)
-    for load in loads:
-        load.wait()
-
-
-def rows_kernel(own_ref, recv_ref, wy_ref, out_ref, scratch):
+    p1 = ones_where(
+        (iota((256, 32), 0) // 128 == iota((256, 32), 1) // 16)
+        & (iota((256, 32), 0) % 16 == iota((256, 32), 1) % 16)
+    )
+    p2 = ones_where(
+        (iota((32, 256), 0) // 8 == iota((32, 256), 1) // 64)
+        & (iota((32, 256), 0) % 8 == iota((32, 256), 1) % 8)
+    )
+    same = (iota((256, 256), 0) // 16) % 8 == (iota((256, 256), 1) // 8) % 8
+    load.wait()
+    full = dot(dot(p1, piece[...]).astype(BF), p2)
+    wy[...] = jnp.where(same, full, 0.0).astype(BF)
+
+
+def rows_kernel(own_ref, recv_ref, wy_ref, after_ref, out_ref, scratch):
+    blocks = []
+    for e in range(4):
+        part = pl.ds(e * 128, 128)
+        blocks.append(dot(jnp.concatenate([own_ref[:, part], recv_ref[:, part]], axis=1), wy_ref[...]))
     for g in range(2):
-        half = pl.ds(g * 256, 256)
-        lhs = jnp.concatenate([own_ref[:, half], recv_ref[:, half]], axis=1)
-        res = dot(lhs, wy_ref[...])
-        for kq in range(4):
-            for kx in range(4):
-                for joct in range(4):
+        for joct in range(4):
+            cols = slice(joct * 64, (joct + 1) * 64)
+            res = jnp.concatenate([blocks[2 * g][:, cols], blocks[2 * g + 1][:, cols]], axis=1)
+            for kq in range(4):
+                for kx in range(4):
                     start = (kx * 4 + joct) * 64 + g * 4 + kq
                     first = (kq * 4 + kx) * 8
-                    scratch[pl.ds(start, 8, stride=8), :] = res[
-                        first : first + 8, joct * 128 : (joct + 1) * 128
-                    ]
+                    scratch[pl.ds(start, 8, stride=8), :] = res[first : first + 8, :]
     out_ref[...] = scratch[...].astype(BF)
 
 
@@ -205,7 +204,7 @@
     out_ref[...] = jnp.broadcast_to(out[None], (128, 8, 128)).reshape(1024, 128).astype(BF)
 
 
-def modes_kernel(modes_ref, wy_ref, planes_ref, after_ref, own_ref, send_ref, scratch):
+def modes_kernel(modes_ref, wy_ref, planes_ref, own_ref, send_ref, scratch):
     scratch[...] = modes_ref[...].astype(F32)
     for g in range(2):
         cols = []
@@ -216,20 +215,19 @@
                     start = (kx * 4 + joct) * 64 + g * 4 + kq
                     pieces.append(scratch[pl.ds(start, 8, stride=8), :])
             cols.append(jnp.concatenate(pieces, axis=0))
-        lhs = jnp.concatenate(cols, axis=1).astype(BF)
-        res = dot(lhs, wy_ref[...], ((1,), (1,))).astype(BF)
-        res = dot(planes_ref[...], res).astype(BF)
-        half = pl.ds(g * 256, 256)
-        own_ref[:, half] = res[:, :256]
-        send_ref[:, half] = res[:, 256:]
-
-
-def point_kernel(field, kron_ref, after_ref, out_ref, grid, sem):
-    copy = pltpu.make_async_copy(field, grid, sem)
-    copy.start()
-    copy.wait()
+        for e in range(2):
+            lanes = slice(e * 64, (e + 1) * 64)
+            lhs = jnp.concatenate([col[:, lanes] for col in cols], axis=1).astype(BF)
+            res = dot(lhs, wy_ref[...], ((1,), (1,))).astype(BF)
+            res = dot(planes_ref[...], res).astype(BF)
+            part = pl.ds((g * 2 + e) * 128, 128)
+            own_ref[:, part] = res[:, :128]
+            send_ref[:, part] = res[:, 128:]
+
+
+def point_kernel(grid_ref, kron_ref, after_ref, out_ref):
     for x in range(X):
-        out_ref[x] = dot(kron_ref[...], grid[:, x].reshape(C * ROWS, DEPTH)).astype(BF)
+        out_ref[x] = dot(kron_ref[...], grid_ref[:, x].reshape(C * ROWS, DEPTH))
 
 
 def grid_kernel(point_ref, own_ref, recv_ref, shift_ref, back_ref, out_ref, stage, sems):
@@ -242,7 +240,7 @@
         for x in range(X):
             part = pl.ds(x * 16, 16)
             modes = jnp.concatenate([own_ref[part, cols], recv_ref[part, cols], shift_ref[:, cols]], axis=0)
-            v = point_ref[x, cols, :].astype(F32) + dot(modes, back_ref[...], ((0,), (0,)))
+            v = point_ref[x, cols, :] + dot(modes, back_ref[...], ((0,), (0,)))
             v = v * jax.nn.sigmoid(v * (a + (a * 0.044715) * (v * v)))
             stage[rows, x] = v.astype(BF).reshape(share, ROWS, DEPTH)
         copies.append(pltpu.make_async_copy(stage.at[rows], out_ref.at[rows], sems.at[q]))
@@ -273,31 +271,36 @@
     dma = pltpu.SemaphoreType.DMA
 
     peer_weight = lax.ppermute(spectral_weight, "c", swap)
-    own, send, wy = call(
+    own, send, back, planes, grid = call(
         analysis_kernel,
         "analysis",
-        (field, front, across, along),
-        (vm(128, 512), vm(128, 512), vm(512, 512)),
+        (field, front, across, back, planes),
+        (vm(128, 512), vm(128, 512), vm(48, DEPTH), vm(128, 128), vm(C, X, ROWS, DEPTH)),
         (
-            vm(C, X, ROWS, DEPTH),
             vm(X * DEPTH, 256),
             vm(DEPTH, 256),
             vm(X, 256, dtype=F32),
-            vm(32, 32),
             dma,
-            dma((3,)),
+            dma((4,)),
         ),
-        (pltpu.HBM,) * 4,
+        (pltpu.HBM,) * 5,
     )
     recv = lax.ppermute(send, "c", swap)
-    parts = call(rows_kernel, "rows", (own, recv, wy), vm(1024, 128), (vm(1024, 128, dtype=F32),))
-    kron, shift, spread, back, planes = call(
+    wy, kron, shift, spread = call(
         tables_kernel,
         "tables",
-        (point_weight, bias.reshape(1, 32), back, planes, parts),
-        (vm(512, 512), vm(16, 512), vm(128, 512), vm(48, DEPTH), vm(128, 128)),
-        (dma((2,)),),
-        (pltpu.VMEM, pltpu.VMEM, pltpu.HBM, pltpu.HBM, pl.ANY),
+        (along, point_weight, bias.reshape(1, 32)),
+        (vm(256, 256), vm(512, 512), vm(16, 512), vm(128, 512)),
+        (vm(32, 32), dma),
+        (pltpu.HBM, pltpu.VMEM, pltpu.VMEM),
+    )
+    parts = call(
+        rows_kernel,
+        "rows",
+        (own, recv, wy, peer_weight),
+        vm(1024, 128),
+        (vm(1024, 128, dtype=F32),),
+        (pltpu.VMEM, pltpu.VMEM, pltpu.VMEM, pl.ANY),
     )
     parts = lax.all_to_all(parts.reshape(128, 8, 128), ("x", "y", "z"), 0, 0, tiled=True)
     mixed = call(
@@ -306,24 +309,23 @@
         (parts.reshape(1024, 128), spectral_weight, peer_weight, spread),
         vm(1024, 128),
     )
-    point = call(
-        point_kernel,
-        "point",
-        (field, kron, mixed),
-        vm(X, C * ROWS, DEPTH),
-        (vm(C, X, ROWS, DEPTH), dma),
-        (pltpu.HBM, pltpu.VMEM, pl.ANY),
-    )
     modes = lax.all_to_all(mixed.reshape(128, 8, 128), ("x", "y", "z"), 0, 0, tiled=True)
     own, send = call(
         modes_kernel,
         "modes",
-        (modes.reshape(1024, 128), wy, planes, point),
+        (modes.reshape(1024, 128), wy, planes),
         (vm(128, 512), vm(128, 512)),
         (vm(1024, 128, dtype=F32),),
-        (pltpu.VMEM, pltpu.VMEM, pltpu.VMEM, pl.ANY),
     )
     recv = lax.ppermute(send, "c", swap)
+    point = call(
+        point_kernel,
+        "point",
+        (grid, kron, own),
+        vm(X, C * ROWS, DEPTH, dtype=F32),
+        (),
+        (pltpu.VMEM, pltpu.VMEM, pl.ANY),
+    )
     return call(
         grid_kernel,
         "grid",

time: 64.6 us -> 63 us (0.975)
  blocking collectives: 0 us -> 46.8 us
  waiting for transfers between devices: 24.2 us -> 0.01 us
  starting transfers between devices: 27.4 us -> 6.44 us
  Pallas kernels: 12.5 us -> 9.42 us
    all_to_all x0 -> x2, blocking collectives: none -> 46.8 us  [the longest x1 27.6 us: shards(): lax.all_to_all(parts.reshape(128, 8, 128), ('x', 'y', 'z'), 0, 0, tiled=T...]
    all_to_all x2 -> x0, waiting for transfers between devices: 22.2 us -> none  [the longest x1 12.3 us: shards(): lax.all_to_all(parts.reshape(128, 8, 128), ('x', 'y', 'z'), 0, 0, tiled=T...]
    all_to_all x2 -> x0, starting transfers between devices: 20.1 us -> none  [the longest x1 13.8 us: shards(): lax.all_to_all(parts.reshape(128, 8, 128), ('x', 'y', 'z'), 0, 0, tiled=T...]
    pallas_call x7, Pallas kernels: 12.5 us -> 9.42 us  [call(): pl.pallas_call(kernel, out_shape=outs, in_specs=[spec(s) for s in spaces]...]
    ppermute x2, waiting for transfers between devices: 1.97 us -> 0.01 us  [shards(): recv = lax.ppermute(send, 'c', swap)]
  transfers between devices with their start and end apart: 5 -> 3, of which waited for: 4 -> 0; matrix products, arithmetic and copies ran while one was open for 0% -> 0% of each run, Pallas kernels for 6% -> 4%
where the time goes in v3:
time: 63 us; the launch traced here: 62.8 us
  blocking collectives  46.8 us (74%)
  Pallas kernels  9.42 us (15%)
  starting transfers between devices  6.44 us (10%)
    all_to_all x1, blocking collectives, shards(): lax.all_to_all(parts.reshape(128, 8, 128), ('x', 'y', 'z'), 0, 0, tiled=T...  27.6 us
    all_to_all x1, blocking collectives, shards(): lax.all_to_all(mixed.reshape(128, 8, 128), ('x', 'y', 'z'), 0, 0, tiled=T...  19.2 us
    pallas_call x7, Pallas kernels, call(): pl.pallas_call(kernel, out_shape=outs, in_specs=[spec(s) for s in spaces]...  9.42 us
    ppermute x2, starting transfers between devices, shards(): recv = lax.ppermute(send, 'c', swap)  6.33 us
  transfers between devices with their start and end apart: 3, of which 0 were waited for; matrix products, arithmetic and copies ran while one was open for 0% of the time, Pallas kernels for 4%

profile of v3, /device:TPU:1, one launch (start us, length us, event | category | flops | bytes accessed | tf_op | source)
XLA Modules:
  0.0 62.8 jit_solution(356348793629720098)
XLA Ops:
  0.0 0.0 copy-start
  0.0 0.0 copy-start.2
  0.0 0.0 copy-start.1
  0.0 2.6 %analysis.1 = (bf16[128,512]{1,0:T(8,128)(2,1)S(1)}, bf16[128,512]{1,0:T(8,128)(2,1)S(1)}, bf16[48,256]{1,0:T(8,128)(2,1)S(1)}, bf16[128,128]{1,0:T(8,128)(2,1)S(1)}, bf16[32,8,16,256]{3,2,1,0:T(8,128)(2,1)S(1)}) custom-call(bf16[32,8,16,256]{3,2,1,0:T(8,128)(2,1)} %field.1, bf16[4,2,256,256]{3,2,1,0:T(8,128)(2,1)} %constant.10.clone.front, ...), custom_call_target="tpu_custom_call" | custom-call | tf_op jit(solution)/shard_map/analysis/pallas_call | solution.py:256
  2.6 3.3 %collective-permute-start = (bf16[128,512]{1,0:T(8,128)(2,1)S(1)}, bf16[128,512]{1,0:T(8,128)(2,1)S(1)}, u32[]{:S(2)}, u32[]{:S(2)}) collective-permute-start(bf16[128,512]{1,0:T(8,128)(2,1)S(1)} %get-tuple-element.19), channel_id=1, source_target_pairs={{0,4},{4,0},{1,5},{5,1},{2,6},{6,2},{3,7},{7,3},{8,12},{12,8},{9,1... | collective-permute-start | bytes 393224 | tf_op jit(solution)/shard_map/ppermute | solution.py:288
  5.9 0.0 copy-done
  5.9 0.1 collective-permute-start.1
  6.0 0.0 copy-done.2
  6.0 0.0 copy-done.1
  6.0 1.3 %tables.1 = (bf16[256,256]{1,0:T(8,128)(2,1)S(1)}, bf16[512,512]{1,0:T(8,128)(2,1)S(1)}, bf16[16,512]{1,0:T(8,128)(2,1)S(1)}, bf16[128,512]{1,0:T(8,128)(2,1)S(1)}) custom-call(bf16[64,32,32]{2,1,0:T(8,128)(2,1)} %constant.12.clone.along, bf16[32,32]{1,0:T(8,128)(2,1)S(1)} %copy-done.1, f32[1,32]{1,0:T(1,128)S(1)} %bitcast.9), custom_call_target="tpu_custom_call" | custom-call | tf_op jit(solution)/shard_map/tables/pallas_call | solution.py:256
  7.3 0.0 collective-permute-done.1.after_ref.peer_ref
  7.4 0.0 collective-permute-done.recv_ref
  7.4 0.4 rows.1
  7.8 27.6 %all_to_all.10 = bf16[128,8,128]{2,1,0:T(8,128)(2,1)S(1)} all-to-all(bf16[128,8,128]{2,1,0:T(8,128)(2,1)S(1)} %bitcast.8), channel_id=1, replica_groups=mesh['z'=8,'y'=4,'c'=2,'x'=4] {'x','y','z'}, dimensions={0} | all-to-all | bytes 524288 | tf_op jit(solution)/shard_map/all_to_all | solution.py:305
  35.4 0.7 %mix.1 = bf16[1024,128]{1,0:T(8,128)(2,1)S(1)} custom-call(bf16[1024,128]{1,0:T(8,128)(2,1)S(1)} %bitcast.5, bf16[4,8,1024]{2,1,0:T(8,128)(2,1)S(1)} %copy-done, bf16[4,8,1024]{2,1,0:T(8,128)(2,1)S(1)} %collective-permute-done.1.after_ref.peer_ref, bf16[128,512]{1,0:T(8,128)(2,1)S(1)} %get-tuple-element.21.spread_ref), custom_call_target="tpu_custom_call" | custom-call | tf_op jit(solution)/shard_map/mix/pallas_call | solution.py:256
  36.2 19.2 %all_to_all.11 = bf16[128,8,128]{2,1,0:T(8,128)(2,1)S(1)} all-to-all(bf16[128,8,128]{2,1,0:T(8,128)(2,1)S(1)} %bitcast.6), channel_id=1, replica_groups=mesh['z'=8,'y'=4,'c'=2,'x'=4] {'x','y','z'}, dimensions={0} | all-to-all | bytes 524288 | tf_op jit(solution)/shard_map/all_to_all | solution.py:312
  55.3 0.9 %modes.1 = (bf16[128,512]{1,0:T(8,128)(2,1)S(1)}, bf16[128,512]{1,0:T(8,128)(2,1)S(1)}) custom-call(bf16[1024,128]{1,0:T(8,128)(2,1)S(1)} %bitcast.7, bf16[256,256]{1,0:T(8,128)(2,1)S(1)} %get-tuple-element.20.wy_ref, bf16[128,128]{1,0:T(8,128)(2,1)S(1)} %get-tuple-element.22.planes_ref), custom_call_target="tpu_custom_call" | custom-call | tf_op jit(solution)/shard_map/modes/pallas_call | solution.py:256
  56.2 3.0 %collective-permute-start.2 = (bf16[128,512]{1,0:T(8,128)(2,1)S(1)}, bf16[128,512]{1,0:T(8,128)(2,1)S(1)}, u32[]{:S(2)}, u32[]{:S(2)}) collective-permute-start(bf16[128,512]{1,0:T(8,128)(2,1)S(1)} %get-tuple-element.24), channel_id=1, source_target_pairs={{0,4},{4,0},{1,5},{5,1},{2,6},{6,2},{3,7},{7,3},{8,12},{12,8},{9,1... | collective-permute-start | bytes 393224 | tf_op jit(solution)/shard_map/ppermute | solution.py:320
  59.3 1.3 %point.1.point_ref = f32[8,512,256]{2,1,0:T(8,128)S(1)} custom-call(bf16[32,8,16,256]{3,2,1,0:T(8,128)(2,1)S(1)} %get-tuple-element.16.grid_ref, bf16[512,512]{1,0:T(8,128)(2,1)S(1)} %get-tuple-element.17.kron_ref, bf16[128,512]{1,0:T(8,128)(2,1)S(1)} %get-tuple-element.23.after_ref.own_ref), custom_call_target="tpu_custom_call" | custom-call | tf_op jit(solution)/shard_map/point/pallas_call | solution.py:256
  60.5 0.0 collective-permute-done.2.recv_ref
  60.5 2.2 %grid.1 = bf16[32,8,16,256]{3,2,1,0:T(8,128)(2,1)} custom-call(f32[8,512,256]{2,1,0:T(8,128)S(1)} %point.1.point_ref, bf16[128,512]{1,0:T(8,128)(2,1)S(1)} %get-tuple-element.23.after_ref.own_ref, bf16[128,512]{1,0:T(8,128)(2,1)S(1)} %collective-permute-done.2.recv_ref, bf16[16,512]{1,0:T(8,128)(2,1)S(1)} %get-tuple-element.25.shift_ref, ...), custom_call_target="tpu_custom_call" | custom-call | tf_op jit(solution)/shard_map/grid/pallas_call | solution.py:256
Async XLA Ops:
  0.0 5.9 %copy-start = (bf16[4,8,1024]{2,1,0:T(8,128)(2,1)S(1)}, bf16[4,8,1024]{2,1,0:T(8,128)(2,1)}, u32[]{:S(2)}) copy-start(bf16[4,8,1024]{2,1,0:T(8,128)(2,1)} %weight_ref.1) | copy-start | bytes 196612
  0.0 6.0 %copy-start.2 = (f32[32]{0:T(128)S(1)}, f32[32]{0:T(128)}, u32[]{:S(2)}) copy-start(f32[32]{0:T(128)} %param.12) | copy-start | bytes 388
  0.0 6.0 %copy-start.1 = (bf16[32,32]{1,0:T(8,128)(2,1)S(1)}, bf16[32,32]{1,0:T(8,128)(2,1)}, u32[]{:S(2)}) copy-start(bf16[32,32]{1,0:T(8,128)(2,1)} %point_ref.1) | copy-start | bytes 6148
  2.6 4.7 %collective-permute-start = (bf16[128,512]{1,0:T(8,128)(2,1)S(1)}, bf16[128,512]{1,0:T(8,128)(2,1)S(1)}, u32[]{:S(2)}, u32[]{:S(2)}) collective-permute-start(bf16[128,512]{1,0:T(8,128)(2,1)S(1)} %get-tuple-element.19), channel_id=1, source_target_pairs={{0,4},{4,0},{1,5},{5,1},{2,6},{6,2},{3,7},{7,3},{8,12},{12,8},{9,1... | collective-permute-start | bytes 393224 | tf_op jit(solution)/shard_map/ppermute | solution.py:288
  5.9 1.4 %collective-permute-start.1 = (bf16[4,8,1024]{2,1,0:T(8,128)(2,1)S(1)}, bf16[4,8,1024]{2,1,0:T(8,128)(2,1)S(1)}, u32[]{:S(2)}, u32[]{:S(2)}) collective-permute-start(bf16[4,8,1024]{2,1,0:T(8,128)(2,1)S(1)} %copy-done), channel_id=1, source_target_pairs={{0,4},{4,0},{1,5},{5,1},{2,6},{6,2},{3,7},{7,3},{8,12},{12,8},{9,1... | collective-permute-start | bytes 196616 | tf_op jit(solution)/shard_map/ppermute | solution.py:273
  56.2 4.3 %collective-permute-start.2 = (bf16[128,512]{1,0:T(8,128)(2,1)S(1)}, bf16[128,512]{1,0:T(8,128)(2,1)S(1)}, u32[]{:S(2)}, u32[]{:S(2)}) collective-permute-start(bf16[128,512]{1,0:T(8,128)(2,1)S(1)} %get-tuple-element.24), channel_id=1, source_target_pairs={{0,4},{4,0},{1,5},{5,1},{2,6},{6,2},{3,7},{7,3},{8,12},{12,8},{9,1... | collective-permute-start | bytes 393224 | tf_op jit(solution)/shard_map/ppermute | solution.py:320

commit v4 on v3

--- a/solution.py
+++ b/solution.py
@@ -56,16 +56,18 @@
             back[chip * 2 + core, :16] = sz[own][:, part]
             back[chip * 2 + core, 16:32] = sz[other][:, part]
             back[chip * 2 + core, 32:35] = 1.0
-    planes = np.zeros((X, 16, 16, X))
-    for m in range(16):
-        planes[:, m, m, :] = ax.T * math.sqrt(N / K)
+    planes = np.zeros((2, X, 4, DX, DX, X, 2, 4))
+    for g in range(2):
+        for q in range(4):
+            for chip in range(DX):
+                planes[g, :, q, chip, chip, :, g, q] = ax.T * math.sqrt(N / K)
     bf = ml_dtypes.bfloat16
     return (
         front.reshape(DX, DC, DEPTH, 256).astype(bf),
         across.astype(np.float32),
         along.astype(bf),
         back.astype(bf),
-        planes.reshape(128, 128).astype(bf),
+        planes.reshape(256, 256).astype(bf),
     )
 
 
@@ -94,37 +96,49 @@
 
 
 def analysis_kernel(
-    field, front, across, back, planes, own, send, back_out, planes_out, grid, weights, base, vectors, field_sem, sems
+    field, front, across, back, planes, along, weight,
+    own, send, back_out, planes_out, along_out, grid,
+    weights, base, vectors, mixing, field_sem, sems,
 ):
+    copy = pltpu.make_async_copy(field, grid, field_sem)
     loads = [
-        pltpu.make_async_copy(front.at[at_chip(), at_core()], base, sems.at[0]),
-        pltpu.make_async_copy(across, vectors, sems.at[1]),
-        pltpu.make_async_copy(back.at[at_chip() * DC + at_core()], back_out, sems.at[2]),
-        pltpu.make_async_copy(planes, planes_out, sems.at[3]),
+        pltpu.make_async_copy(source, target, sems.at[at])
+        for at, (source, target) in enumerate(
+            (
+                (front.at[at_chip(), at_core()], base),
+                (across, vectors),
+                (weight, mixing),
+                (back.at[at_chip() * DC + at_core()], back_out),
+                (planes, planes_out),
+                (along.at[at_rows()], along_out),
+            )
+        )
     ]
-    copy = pltpu.make_async_copy(field, grid, field_sem)
     loads[0].start()
     loads[1].start()
     copy.start()
-    loads[2].start()
-    loads[3].start()
+    for load in loads[2:]:
+        load.start()
     loads[0].wait()
     loads[1].wait()
     wide = base[...].astype(F32)
     for x in range(X):
         weights[pl.ds(x * DEPTH, DEPTH), :] = (wide * vectors[pl.ds(x, 1), :]).astype(BF)
+    for load in loads[2:]:
+        load.wait()
+    given = mixing[...].reshape(32, 1024)
+    send[128:160, :] = given[:, :512]
+    send[160:192, :] = given[:, 512:]
     copy.wait()
     lhs = jnp.concatenate([grid[:, x].reshape(C * ROWS, DEPTH) for x in range(X)], axis=1)
     res = dot(lhs, weights[...]).T.astype(BF)
     own[...] = res[:128]
-    send[...] = res[128:]
-    loads[2].wait()
-    loads[3].wait()
-
-
-def tables_kernel(along, point_ref, bias_ref, wy, kron_ref, shift_ref, spread_ref, piece, sem):
-    load = pltpu.make_async_copy(along.at[at_rows()], piece, sem)
-    load.start()
+    send[:128, :] = res[128:]
+
+
+def tables_kernel(along_ref, point_ref, bias_ref, wy, order_ref, kron_ref, shift_ref):
+    to, source = iota((256, 256), 0), iota((256, 256), 1)
+    order_ref[...] = ones_where(source == (to // 4 % 2) * 128 + (to % 4) * 32 + to // 8)
     e1 = ones_where(iota((512, 32), 0) // 16 == iota((512, 32), 1))
     e2 = ones_where(iota((32, 512), 0) == iota((32, 512), 1) // 16)
     wide = dot(dot(e1, point_ref[...], ((1,), (1,))).astype(BF), e2)
@@ -137,7 +151,6 @@
     row = iota((16, 32), 0)
     parts = jnp.where(row == 0, b1, jnp.where(row == 1, b2, jnp.where(row == 2, b3, 0.0)))
     shift_ref[...] = dot(parts.astype(BF), e2).astype(BF)
-    spread_ref[...] = ones_where(iota((128, 512), 0) // 8 == iota((128, 512), 1) // 32)
     p1 = ones_where(
         (iota((256, 32), 0) // 128 == iota((256, 32), 1) // 16)
         & (iota((256, 32), 0) % 16 == iota((256, 32), 1) % 16)
@@ -147,29 +160,27 @@
         & (iota((32, 256), 0) % 8 == iota((32, 256), 1) % 8)
     )
     same = (iota((256, 256), 0) // 16) % 8 == (iota((256, 256), 1) // 8) % 8
-    load.wait()
-    full = dot(dot(p1, piece[...]).astype(BF), p2)
+    full = dot(dot(p1, along_ref[...]).astype(BF), p2)
     wy[...] = jnp.where(same, full, 0.0).astype(BF)
 
 
-def rows_kernel(own_ref, recv_ref, wy_ref, after_ref, out_ref, scratch):
+def rows_kernel(own_ref, recv_ref, wy_ref, order_ref, out_ref, peer_out):
     blocks = []
-    for e in range(4):
-        part = pl.ds(e * 128, 128)
-        blocks.append(dot(jnp.concatenate([own_ref[:, part], recv_ref[:, part]], axis=1), wy_ref[...]))
-    for g in range(2):
-        for joct in range(4):
-            cols = slice(joct * 64, (joct + 1) * 64)
-            res = jnp.concatenate([blocks[2 * g][:, cols], blocks[2 * g + 1][:, cols]], axis=1)
-            for kq in range(4):
-                for kx in range(4):
-                    start = (kx * 4 + joct) * 64 + g * 4 + kq
-                    first = (kq * 4 + kx) * 8
-                    scratch[pl.ds(start, 8, stride=8), :] = res[first : first + 8, :]
-    out_ref[...] = scratch[...].astype(BF)
-
-
-def mix_kernel(parts_ref, weight_ref, peer_ref, spread_ref, out_ref):
+    for e in range(2):
+        halves = []
+        for g in range(2):
+            part = pl.ds((g * 2 + e) * 128, 128)
+            halves.append(dot(jnp.concatenate([own_ref[:, part], recv_ref[:128, part]], axis=1), wy_ref[...]))
+        blocks.append(dot(order_ref[...], jnp.concatenate(halves, axis=0).astype(BF)))
+    for joct in range(4):
+        cols = slice(joct * 64, (joct + 1) * 64)
+        res = jnp.concatenate([blocks[0][:, cols], blocks[1][:, cols]], axis=1)
+        for to in range(32):
+            out_ref[pl.ds((to * 4 + joct) * 8, 8), :] = res[to * 8 : (to + 1) * 8, :].astype(BF)
+    peer_out[...] = recv_ref[128:192, :]
+
+
+def mix_kernel(parts_ref, weight_ref, peer_ref, out_ref):
     core = at_core()
     s = jnp.sum(parts_ref[...].astype(F32).reshape(128, 8, 128), axis=0)
     row = iota((8, 128), 0)
@@ -181,12 +192,11 @@
     s64 = jnp.where(keep, s64, 0.0)
     high = s64.astype(BF)
     low = (s64 - high.astype(F32)).astype(BF)
-    spread = spread_ref[...]
+    spread = ones_where(iota((128, 512), 0) // 8 == iota((128, 512), 1) // 32)
     halves = [dot(high[:, part], spread) + dot(low[:, part], spread) for part in (slice(0, 128), slice(128, 256))]
     wide = jnp.concatenate(halves, axis=1)
-    weight = jnp.concatenate(
-        [weight_ref[...].astype(F32).reshape(32, 1024), peer_ref[...].astype(F32).reshape(32, 1024)], axis=0
-    )
+    peer = jnp.concatenate([peer_ref[:32, :], peer_ref[32:, :]], axis=1)
+    weight = jnp.concatenate([weight_ref[...].reshape(32, 1024), peer], axis=0).astype(F32)
     prod = wide * weight
     total = prod[:, 0:128]
     for part in range(1, 8):
@@ -204,25 +214,21 @@
     out_ref[...] = jnp.broadcast_to(out[None], (128, 8, 128)).reshape(1024, 128).astype(BF)
 
 
-def modes_kernel(modes_ref, wy_ref, planes_ref, own_ref, send_ref, scratch):
-    scratch[...] = modes_ref[...].astype(F32)
-    for g in range(2):
-        cols = []
-        for joct in range(4):
-            pieces = []
-            for kq in range(4):
-                for kx in range(4):
-                    start = (kx * 4 + joct) * 64 + g * 4 + kq
-                    pieces.append(scratch[pl.ds(start, 8, stride=8), :])
-            cols.append(jnp.concatenate(pieces, axis=0))
-        for e in range(2):
-            lanes = slice(e * 64, (e + 1) * 64)
-            lhs = jnp.concatenate([col[:, lanes] for col in cols], axis=1).astype(BF)
-            res = dot(lhs, wy_ref[...], ((1,), (1,))).astype(BF)
-            res = dot(planes_ref[...], res).astype(BF)
+def modes_kernel(modes_ref, wy_ref, planes_ref, own_ref, send_ref):
+    for e in range(2):
+        lanes = slice(e * 64, (e + 1) * 64)
+        rows = []
+        for kx in range(4):
+            for i in range(8):
+                at = ((kx * 8 + i) * 4) * 8
+                cols = [modes_ref[pl.ds(at + joct * 8, 8), :][:, lanes] for joct in range(4)]
+                rows.append(jnp.concatenate(cols, axis=1))
+        res = dot(jnp.concatenate(rows, axis=0), wy_ref[...], ((1,), (1,))).astype(BF)
+        res = dot(planes_ref[...], res).astype(BF)
+        for g in range(2):
             part = pl.ds((g * 2 + e) * 128, 128)
-            own_ref[:, part] = res[:, :128]
-            send_ref[:, part] = res[:, 128:]
+            own_ref[:, part] = res[g * 128 : (g + 1) * 128, :128]
+            send_ref[:, part] = res[g * 128 : (g + 1) * 128, 128:]
 
 
 def point_kernel(grid_ref, kron_ref, after_ref, out_ref):
@@ -270,52 +276,47 @@
     vm = lambda *shape, dtype=BF: pltpu.VMEM(shape, dtype)
     dma = pltpu.SemaphoreType.DMA
 
-    peer_weight = lax.ppermute(spectral_weight, "c", swap)
-    own, send, back, planes, grid = call(
+    own, send, back, planes, along, grid = call(
         analysis_kernel,
         "analysis",
-        (field, front, across, back, planes),
-        (vm(128, 512), vm(128, 512), vm(48, DEPTH), vm(128, 128), vm(C, X, ROWS, DEPTH)),
+        (field, front, across, back, planes, along, spectral_weight),
+        (vm(128, 512), vm(192, 512), vm(48, DEPTH), vm(256, 256), vm(32, 32), vm(C, X, ROWS, DEPTH)),
         (
             vm(X * DEPTH, 256),
             vm(DEPTH, 256),
             vm(X, 256, dtype=F32),
+            vm(4, 8, 1024),
             dma,
-            dma((4,)),
+            dma((6,)),
         ),
-        (pltpu.HBM,) * 5,
+        (pltpu.HBM,) * 7,
     )
     recv = lax.ppermute(send, "c", swap)
-    wy, kron, shift, spread = call(
+    wy, order, kron, shift = call(
         tables_kernel,
         "tables",
         (along, point_weight, bias.reshape(1, 32)),
-        (vm(256, 256), vm(512, 512), vm(16, 512), vm(128, 512)),
-        (vm(32, 32), dma),
-        (pltpu.HBM, pltpu.VMEM, pltpu.VMEM),
-    )
-    parts = call(
+        (vm(256, 256), vm(256, 256), vm(512, 512), vm(16, 512)),
+    )
+    parts, peer_weight = call(
         rows_kernel,
         "rows",
-        (own, recv, wy, peer_weight),
-        vm(1024, 128),
-        (vm(1024, 128, dtype=F32),),
-        (pltpu.VMEM, pltpu.VMEM, pltpu.VMEM, pl.ANY),
-    )
-    parts = lax.all_to_all(parts.reshape(128, 8, 128), ("x", "y", "z"), 0, 0, tiled=True)
+        (own, recv, wy, order),
+        (vm(1024, 128), vm(64, 512)),
+    )
+    parts = lax.all_to_all(parts.reshape(128, 8, 128), ("x", "z", "y"), 0, 0, tiled=True)
     mixed = call(
         mix_kernel,
         "mix",
-        (parts.reshape(1024, 128), spectral_weight, peer_weight, spread),
+        (parts.reshape(1024, 128), spectral_weight, peer_weight),
         vm(1024, 128),
     )
-    modes = lax.all_to_all(mixed.reshape(128, 8, 128), ("x", "y", "z"), 0, 0, tiled=True)
+    modes = lax.all_to_all(mixed.reshape(128, 8, 128), ("x", "z", "y"), 0, 0, tiled=True)
     own, send = call(
         modes_kernel,
         "modes",
         (modes.reshape(1024, 128), wy, planes),
         (vm(128, 512), vm(128, 512)),
-        (vm(1024, 128, dtype=F32),),
     )
     recv = lax.ppermute(send, "c", swap)
     point = call(

time: 63 us -> 61.7 us (0.979)
  blocking collectives: 46.8 us -> 45.2 us
  Pallas kernels: 9.42 us -> 8.65 us
    all_to_all x2, blocking collectives: 46.8 us -> 45.2 us  [the longest x1 26.5 us: shards(): lax.all_to_all(parts.reshape(128, 8, 128), ('x', 'z', 'y'), 0, 0, tiled=T...]
    pallas_call x7, Pallas kernels: 9.42 us -> 8.65 us  [call(): pl.pallas_call(kernel, out_shape=outs, in_specs=[spec(s) for s in spaces]...]
    ppermute x2, starting transfers between devices: 6.33 us -> 7.07 us  [shards(): recv = lax.ppermute(send, 'c', swap)]
  transfers between devices with their start and end apart: 3 -> 2, of which waited for: 0 -> 1; matrix products, arithmetic and copies ran while one was open for 0% -> 0% of each run, Pallas kernels for 4% -> 3%
where the time goes in v4:
time: 61.7 us; the launch traced here: 61.5 us
  blocking collectives  45.2 us (73%)
  Pallas kernels  8.65 us (14%)
  starting transfers between devices  7.07 us (11%)
    all_to_all x1, blocking collectives, shards(): lax.all_to_all(parts.reshape(128, 8, 128), ('x', 'z', 'y'), 0, 0, tiled=T...  26.5 us
    all_to_all x1, blocking collectives, shards(): lax.all_to_all(mixed.reshape(128, 8, 128), ('x', 'z', 'y'), 0, 0, tiled=T...  18.7 us
    pallas_call x7, Pallas kernels, call(): pl.pallas_call(kernel, out_shape=outs, in_specs=[spec(s) for s in spaces]...  8.65 us
    ppermute x2, starting transfers between devices, shards(): recv = lax.ppermute(send, 'c', swap)  7.07 us
  transfers between devices with their start and end apart: 2, of which 1 were waited for; matrix products, arithmetic and copies ran while one was open for 0% of the time, Pallas kernels for 3%

profile of v4, /device:TPU:1, one launch (start us, length us, event | category | flops | bytes accessed | tf_op | source)
XLA Modules:
  0.0 61.5 jit_solution(10447263206496185576)
XLA Ops:
  0.0 0.0 copy-start
  0.0 0.0 copy-start.2
  0.0 0.0 copy-start.1
  0.0 2.6 %analysis.1 = (bf16[128,512]{1,0:T(8,128)(2,1)S(1)}, bf16[192,512]{1,0:T(8,128)(2,1)S(1)}, bf16[48,256]{1,0:T(8,128)(2,1)S(1)}, bf16[256,256]{1,0:T(8,128)(2,1)S...) custom-call(bf16[32,8,16,256]{3,2,1,0:T(8,128)(2,1)} %field.1, ...), custom_call_target="tpu_custom_call" | custom-call | tf_op jit(solution)/shard_map/analysis/pallas_call | solution.py:262
  2.6 3.3 %collective-permute-start = (bf16[192,512]{1,0:T(8,128)(2,1)S(1)}, bf16[192,512]{1,0:T(8,128)(2,1)S(1)}, u32[]{:S(2)}, u32[]{:S(2)}) collective-permute-start(bf16[192,512]{1,0:T(8,128)(2,1)S(1)} %get-tuple-element.23), channel_id=1, source_target_pairs={{0,4},{4,0},{1,5},{5,1},{2,6},{6,2},{3,7},{7,3},{8,12},{12,8},{9,1... | collective-permute-start | bytes 589832 | tf_op jit(solution)/shard_map/ppermute | solution.py:294
  5.9 0.0 copy-done.2
  5.9 0.0 copy-done.1
  6.0 0.6 tables.1
  6.5 0.5 collective-permute-done.recv_ref
  7.0 0.5 rows.1
  7.6 26.5 %all_to_all.10 = bf16[128,8,128]{2,1,0:T(8,128)(2,1)S(1)} all-to-all(bf16[128,8,128]{2,1,0:T(8,128)(2,1)S(1)} %bitcast.8), channel_id=1, replica_groups=mesh['z'=8,'y'=4,'c'=2,'x'=4] {'x','z','y'}, dimensions={0} | all-to-all | bytes 524288 | tf_op jit(solution)/shard_map/all_to_all | solution.py:307
  34.1 0.0 copy-done
  34.1 0.8 %mix.1 = bf16[1024,128]{1,0:T(8,128)(2,1)S(1)} custom-call(bf16[1024,128]{1,0:T(8,128)(2,1)S(1)} %bitcast.6, bf16[4,8,1024]{2,1,0:T(8,128)(2,1)S(1)} %copy-done, bf16[64,512]{1,0:T(8,128)(2,1)S(1)} %get-tuple-element.27.peer_ref), custom_call_target="tpu_custom_call" | custom-call | tf_op jit(solution)/shard_map/mix/pallas_call | solution.py:262
  34.9 18.7 %all_to_all.11 = bf16[128,8,128]{2,1,0:T(8,128)(2,1)S(1)} all-to-all(bf16[128,8,128]{2,1,0:T(8,128)(2,1)S(1)} %bitcast.7), channel_id=1, replica_groups=mesh['z'=8,'y'=4,'c'=2,'x'=4] {'x','z','y'}, dimensions={0} | all-to-all | bytes 524288 | tf_op jit(solution)/shard_map/all_to_all | solution.py:314
  53.6 0.7 %modes.1 = (bf16[128,512]{1,0:T(8,128)(2,1)S(1)}, bf16[128,512]{1,0:T(8,128)(2,1)S(1)}) custom-call(bf16[1024,128]{1,0:T(8,128)(2,1)S(1)} %bitcast.5, bf16[256,256]{1,0:T(8,128)(2,1)S(1)} %get-tuple-element.24.wy_ref, bf16[256,256]{1,0:T(8,128)(2,1)S(1)} %get-tuple-element.28.planes_ref), custom_call_target="tpu_custom_call" | custom-call | tf_op jit(solution)/shard_map/modes/pallas_call | solution.py:262
  54.2 3.8 %collective-permute-start.1 = (bf16[128,512]{1,0:T(8,128)(2,1)S(1)}, bf16[128,512]{1,0:T(8,128)(2,1)S(1)}, u32[]{:S(2)}, u32[]{:S(2)}) collective-permute-start(bf16[128,512]{1,0:T(8,128)(2,1)S(1)} %get-tuple-element.30), channel_id=1, source_target_pairs={{0,4},{4,0},{1,5},{5,1},{2,6},{6,2},{3,7},{7,3},{8,12},{12,8},{9,1... | collective-permute-start | bytes 393224 | tf_op jit(solution)/shard_map/ppermute | solution.py:321
  58.0 1.2 %point.1.point_ref = f32[8,512,256]{2,1,0:T(8,128)S(1)} custom-call(bf16[32,8,16,256]{3,2,1,0:T(8,128)(2,1)S(1)} %get-tuple-element.19.grid_ref, bf16[512,512]{1,0:T(8,128)(2,1)S(1)} %get-tuple-element.21.kron_ref, bf16[128,512]{1,0:T(8,128)(2,1)S(1)} %get-tuple-element.29.after_ref.own_ref), custom_call_target="tpu_custom_call" | custom-call | tf_op jit(solution)/shard_map/point/pallas_call | solution.py:262
  59.3 0.0 collective-permute-done.1.recv_ref
  59.3 2.2 %grid.1 = bf16[32,8,16,256]{3,2,1,0:T(8,128)(2,1)} custom-call(f32[8,512,256]{2,1,0:T(8,128)S(1)} %point.1.point_ref, bf16[128,512]{1,0:T(8,128)(2,1)S(1)} %get-tuple-element.29.after_ref.own_ref, bf16[128,512]{1,0:T(8,128)(2,1)S(1)} %collective-permute-done.1.recv_ref, bf16[16,512]{1,0:T(8,128)(2,1)S(1)} %get-tuple-element.31.shift_ref, ...), custom_call_target="tpu_custom_call" | custom-call | tf_op jit(solution)/shard_map/grid/pallas_call | solution.py:262
Async XLA Ops:
  0.0 34.1 %copy-start = (bf16[4,8,1024]{2,1,0:T(8,128)(2,1)S(1)}, bf16[4,8,1024]{2,1,0:T(8,128)(2,1)}, u32[]{:S(2)}) copy-start(bf16[4,8,1024]{2,1,0:T(8,128)(2,1)} %weight_ref.1) | copy-start | bytes 196612
  0.0 5.9 %copy-start.2 = (f32[32]{0:T(128)S(1)}, f32[32]{0:T(128)}, u32[]{:S(2)}) copy-start(f32[32]{0:T(128)} %param.12) | copy-start | bytes 388
  0.0 5.9 %copy-start.1 = (bf16[32,32]{1,0:T(8,128)(2,1)S(1)}, bf16[32,32]{1,0:T(8,128)(2,1)}, u32[]{:S(2)}) copy-start(bf16[32,32]{1,0:T(8,128)(2,1)} %point_ref.1) | copy-start | bytes 6148
  2.6 4.4 %collective-permute-start = (bf16[192,512]{1,0:T(8,128)(2,1)S(1)}, bf16[192,512]{1,0:T(8,128)(2,1)S(1)}, u32[]{:S(2)}, u32[]{:S(2)}) collective-permute-start(bf16[192,512]{1,0:T(8,128)(2,1)S(1)} %get-tuple-element.23), channel_id=1, source_target_pairs={{0,4},{4,0},{1,5},{5,1},{2,6},{6,2},{3,7},{7,3},{8,12},{12,8},{9,1... | collective-permute-start | bytes 589832 | tf_op jit(solution)/shard_map/ppermute | solution.py:294
  54.2 5.0 %collective-permute-start.1 = (bf16[128,512]{1,0:T(8,128)(2,1)S(1)}, bf16[128,512]{1,0:T(8,128)(2,1)S(1)}, u32[]{:S(2)}, u32[]{:S(2)}) collective-permute-start(bf16[128,512]{1,0:T(8,128)(2,1)S(1)} %get-tuple-element.30), channel_id=1, source_target_pairs={{0,4},{4,0},{1,5},{5,1},{2,6},{6,2},{3,7},{7,3},{8,12},{12,8},{9,1... | collective-permute-start | bytes 393224 | tf_op jit(solution)/shard_map/ppermute | solution.py:321

commit v5 on v4

--- a/solution.py
+++ b/solution.py
@@ -139,10 +139,10 @@
 def tables_kernel(along_ref, point_ref, bias_ref, wy, order_ref, kron_ref, shift_ref):
     to, source = iota((256, 256), 0), iota((256, 256), 1)
     order_ref[...] = ones_where(source == (to // 4 % 2) * 128 + (to % 4) * 32 + to // 8)
-    e1 = ones_where(iota((512, 32), 0) // 16 == iota((512, 32), 1))
-    e2 = ones_where(iota((32, 512), 0) == iota((32, 512), 1) // 16)
+    e1 = ones_where(iota((256, 32), 0) // 8 == iota((256, 32), 1))
+    e2 = ones_where(iota((32, 256), 0) == iota((32, 256), 1) // 8)
     wide = dot(dot(e1, point_ref[...], ((1,), (1,))).astype(BF), e2)
-    same = iota((512, 512), 0) % 16 == iota((512, 512), 1) % 16
+    same = iota((256, 256), 0) % 8 == iota((256, 256), 1) % 8
     kron_ref[...] = jnp.where(same, wide, 0.0).astype(BF)
     b = jnp.broadcast_to(bias_ref[...], (16, 32))
     b1 = b.astype(BF).astype(F32)
@@ -150,33 +150,33 @@
     b3 = b - b1 - b2
     row = iota((16, 32), 0)
     parts = jnp.where(row == 0, b1, jnp.where(row == 1, b2, jnp.where(row == 2, b3, 0.0)))
-    shift_ref[...] = dot(parts.astype(BF), e2).astype(BF)
+    e3 = ones_where(iota((32, 512), 0) == iota((32, 512), 1) // 16)
+    shift_ref[...] = dot(parts.astype(BF), e3).astype(BF)
     p1 = ones_where(
-        (iota((256, 32), 0) // 128 == iota((256, 32), 1) // 16)
-        & (iota((256, 32), 0) % 16 == iota((256, 32), 1) % 16)
+        (iota((512, 32), 0) // 256 == iota((512, 32), 1) // 16)
+        & (iota((512, 32), 0) % 16 == iota((512, 32), 1) % 16)
     )
     p2 = ones_where(
-        (iota((32, 256), 0) // 8 == iota((32, 256), 1) // 64)
-        & (iota((32, 256), 0) % 8 == iota((32, 256), 1) % 8)
-    )
-    same = (iota((256, 256), 0) // 16) % 8 == (iota((256, 256), 1) // 8) % 8
+        (iota((32, 512), 0) // 8 == iota((32, 512), 1) // 128)
+        & (iota((32, 512), 0) % 8 == iota((32, 512), 1) % 8)
+    )
+    same = (iota((512, 512), 0) // 16) % 16 == (iota((512, 512), 1) // 8) % 16
     full = dot(dot(p1, along_ref[...]).astype(BF), p2)
     wy[...] = jnp.where(same, full, 0.0).astype(BF)
 
 
 def rows_kernel(own_ref, recv_ref, wy_ref, order_ref, out_ref, peer_out):
-    blocks = []
-    for e in range(2):
-        halves = []
-        for g in range(2):
-            part = pl.ds((g * 2 + e) * 128, 128)
-            halves.append(dot(jnp.concatenate([own_ref[:, part], recv_ref[:128, part]], axis=1), wy_ref[...]))
-        blocks.append(dot(order_ref[...], jnp.concatenate(halves, axis=0).astype(BF)))
-    for joct in range(4):
-        cols = slice(joct * 64, (joct + 1) * 64)
-        res = jnp.concatenate([blocks[0][:, cols], blocks[1][:, cols]], axis=1)
-        for to in range(32):
-            out_ref[pl.ds((to * 4 + joct) * 8, 8), :] = res[to * 8 : (to + 1) * 8, :].astype(BF)
+    halves = []
+    for g in range(2):
+        part = pl.ds(g * 256, 256)
+        halves.append(jnp.concatenate([own_ref[:, part], recv_ref[:128, part]], axis=1))
+    lhs = dot(order_ref[...], jnp.concatenate(halves, axis=0)).astype(BF)
+    res = dot(lhs, wy_ref[...])
+    for to in range(32):
+        for joct in range(4):
+            out_ref[pl.ds((to * 4 + joct) * 8, 8), :] = res[
+                to * 8 : (to + 1) * 8, joct * 128 : (joct + 1) * 128
+            ].astype(BF)
     peer_out[...] = recv_ref[128:192, :]
 
 
@@ -192,48 +192,50 @@
     s64 = jnp.where(keep, s64, 0.0)
     high = s64.astype(BF)
     low = (s64 - high.astype(F32)).astype(BF)
+    parts = jnp.concatenate([high, low], axis=0)
     spread = ones_where(iota((128, 512), 0) // 8 == iota((128, 512), 1) // 32)
-    halves = [dot(high[:, part], spread) + dot(low[:, part], spread) for part in (slice(0, 128), slice(128, 256))]
-    wide = jnp.concatenate(halves, axis=1)
     peer = jnp.concatenate([peer_ref[:32, :], peer_ref[32:, :]], axis=1)
     weight = jnp.concatenate([weight_ref[...].reshape(32, 1024), peer], axis=0).astype(F32)
-    prod = wide * weight
-    total = prod[:, 0:128]
-    for part in range(1, 8):
-        total = total + prod[:, part * 128 : (part + 1) * 128]
+    total = jnp.zeros((64, 128), F32)
+    for g in range(2):
+        wide = dot(parts[:, g * 128 : (g + 1) * 128], spread)
+        prod = (wide[:64] + wide[64:]) * weight[:, g * 512 : (g + 1) * 512]
+        for part in range(4):
+            total = total + prod[:, part * 128 : (part + 1) * 128]
     total = total + pltpu.roll(total, 64, 1)
     total = total + pltpu.roll(total, 32, 1)
     mixed = total.astype(BF)
     q, col = iota((128, 256), 0), iota((128, 256), 1)
     place = ones_where(q == (col // 128) * 16 + (col % 128) // 8)
     placed = dot(mixed, place)
-    placed = jnp.where(iota((64, 256), 1) % 8 == iota((64, 256), 0) // 8, placed, 0.0).astype(BF)
-    take = ones_where(iota((8, 64), 0) % 4 == iota((8, 64), 1) % 4)
-    both = dot(take, placed)
-    out = jnp.where(iota((8, 128), 0) < 4, both[:, :128], both[:, 128:])
-    out_ref[...] = jnp.broadcast_to(out[None], (128, 8, 128)).reshape(1024, 128).astype(BF)
+    placed = jnp.where(iota((64, 256), 1) % 8 == iota((64, 256), 0) // 8, placed, 0.0)
+    both = placed[:8]
+    for j in range(1, 8):
+        both = both + placed[j * 8 : (j + 1) * 8]
+    both = both + pltpu.roll(both, 4, 0)
+    out = jnp.where(iota((8, 128), 0) < 4, both[:, :128], both[:, 128:]).astype(BF)
+    out_ref[...] = jnp.broadcast_to(out[None], (128, 8, 128)).reshape(1024, 128)
 
 
 def modes_kernel(modes_ref, wy_ref, planes_ref, own_ref, send_ref):
-    for e in range(2):
-        lanes = slice(e * 64, (e + 1) * 64)
-        rows = []
-        for kx in range(4):
-            for i in range(8):
-                at = ((kx * 8 + i) * 4) * 8
-                cols = [modes_ref[pl.ds(at + joct * 8, 8), :][:, lanes] for joct in range(4)]
-                rows.append(jnp.concatenate(cols, axis=1))
-        res = dot(jnp.concatenate(rows, axis=0), wy_ref[...], ((1,), (1,))).astype(BF)
-        res = dot(planes_ref[...], res).astype(BF)
-        for g in range(2):
-            part = pl.ds((g * 2 + e) * 128, 128)
-            own_ref[:, part] = res[g * 128 : (g + 1) * 128, :128]
-            send_ref[:, part] = res[g * 128 : (g + 1) * 128, 128:]
+    rows = []
+    for to in range(32):
+        cols = [modes_ref[pl.ds((to * 4 + joct) * 8, 8), :] for joct in range(4)]
+        rows.append(jnp.concatenate(cols, axis=1))
+    res = dot(jnp.concatenate(rows, axis=0), wy_ref[...], ((1,), (1,))).astype(BF)
+    res = dot(planes_ref[...], res).astype(BF)
+    for g in range(2):
+        part = pl.ds(g * 256, 256)
+        own_ref[:, part] = res[g * 128 : (g + 1) * 128, :256]
+        send_ref[:, part] = res[g * 128 : (g + 1) * 128, 256:]
 
 
 def point_kernel(grid_ref, kron_ref, after_ref, out_ref):
     for x in range(X):
-        out_ref[x] = dot(kron_ref[...], grid_ref[:, x].reshape(C * ROWS, DEPTH))
+        for half in range(2):
+            part = slice(half * 8, half * 8 + 8)
+            res = dot(kron_ref[...], grid_ref[:, x, part, :].reshape(C * 8, DEPTH))
+            out_ref[x, :, part, :] = res.reshape(C, 8, DEPTH)
 
 
 def grid_kernel(point_ref, own_ref, recv_ref, shift_ref, back_ref, out_ref, stage, sems):
@@ -246,9 +248,10 @@
         for x in range(X):
             part = pl.ds(x * 16, 16)
             modes = jnp.concatenate([own_ref[part, cols], recv_ref[part, cols], shift_ref[:, cols]], axis=0)
-            v = point_ref[x, cols, :] + dot(modes, back_ref[...], ((0,), (0,)))
-            v = v * jax.nn.sigmoid(v * (a + (a * 0.044715) * (v * v)))
-            stage[rows, x] = v.astype(BF).reshape(share, ROWS, DEPTH)
+            v = point_ref[x, rows].reshape(share * ROWS, DEPTH) + dot(modes, back_ref[...], ((0,), (0,)))
+            v = v.astype(BF)
+            v = v * jax.nn.sigmoid(v * (jnp.asarray(a, BF) + jnp.asarray(a * 0.044715, BF) * (v * v)))
+            stage[rows, x] = v.reshape(share, ROWS, DEPTH)
         copies.append(pltpu.make_async_copy(stage.at[rows], out_ref.at[rows], sems.at[q]))
         copies[-1].start()
     for copy in copies:
@@ -296,7 +299,7 @@
         tables_kernel,
         "tables",
         (along, point_weight, bias.reshape(1, 32)),
-        (vm(256, 256), vm(256, 256), vm(512, 512), vm(16, 512)),
+        (vm(512, 512), vm(256, 256), vm(256, 256), vm(16, 512)),
     )
     parts, peer_weight = call(
         rows_kernel,
@@ -323,7 +326,7 @@
         point_kernel,
         "point",
         (grid, kron, own),
-        vm(X, C * ROWS, DEPTH, dtype=F32),
+        vm(X, C, ROWS, DEPTH, dtype=F32),
         (),
         (pltpu.VMEM, pltpu.VMEM, pl.ANY),
     )

time: 61.7 us -> 60.6 us (0.982)
  Pallas kernels: 8.65 us -> 7.24 us
    pallas_call x7, Pallas kernels: 8.65 us -> 7.24 us  [call(): pl.pallas_call(kernel, out_shape=outs, in_specs=[spec(s) for s in spaces]...]
  transfers between devices with their start and end apart: 2 -> 2, of which waited for: 1 -> 2; matrix products, arithmetic and copies ran while one was open for 0% -> 0% of each run, Pallas kernels for 3% -> 2%
where the time goes in v5:
time: 60.6 us; the launch traced here: 60.5 us
  blocking collectives  45.2 us (75%)
  Pallas kernels  7.24 us (12%)
  starting transfers between devices  7.07 us (12%)
  waiting for transfers between devices  0.87 us (1%)
    all_to_all x1, blocking collectives, shards(): lax.all_to_all(parts.reshape(128, 8, 128), ('x', 'z', 'y'), 0, 0, tiled=T...  26.5 us
    all_to_all x1, blocking collectives, shards(): lax.all_to_all(mixed.reshape(128, 8, 128), ('x', 'z', 'y'), 0, 0, tiled=T...  18.7 us
    pallas_call x7, Pallas kernels, call(): pl.pallas_call(kernel, out_shape=outs, in_specs=[spec(s) for s in spaces]...  7.24 us
    ppermute x2, starting transfers between devices, shards(): recv = lax.ppermute(send, 'c', swap)  7.07 us
  transfers between devices with their start and end apart: 2, of which 2 were waited for; matrix products, arithmetic and copies ran while one was open for 0% of the time, Pallas kernels for 2%

profile of v5, /device:TPU:1, one launch (start us, length us, event | category | flops | bytes accessed | tf_op | source)
XLA Modules:
  0.0 60.5 jit_solution(2275580569288967402)
XLA Ops:
  0.0 0.0 copy-start
  0.0 0.0 copy-start.2
  0.0 0.0 copy-start.1
  0.0 2.6 %analysis.1 = (bf16[128,512]{1,0:T(8,128)(2,1)S(1)}, bf16[192,512]{1,0:T(8,128)(2,1)S(1)}, bf16[48,256]{1,0:T(8,128)(2,1)S(1)}, bf16[256,256]{1,0:T(8,128)(2,1)S...) custom-call(bf16[32,8,16,256]{3,2,1,0:T(8,128)(2,1)} %field.1, ...), custom_call_target="tpu_custom_call" | custom-call | tf_op jit(solution)/shard_map/analysis/pallas_call | solution.py:265
  2.6 3.3 %collective-permute-start = (bf16[192,512]{1,0:T(8,128)(2,1)S(1)}, bf16[192,512]{1,0:T(8,128)(2,1)S(1)}, u32[]{:S(2)}, u32[]{:S(2)}) collective-permute-start(bf16[192,512]{1,0:T(8,128)(2,1)S(1)} %get-tuple-element.23), channel_id=1, source_target_pairs={{0,4},{4,0},{1,5},{5,1},{2,6},{6,2},{3,7},{7,3},{8,12},{12,8},{9,1... | collective-permute-start | bytes 589832 | tf_op jit(solution)/shard_map/ppermute | solution.py:297
  5.9 0.0 copy-done.2
  5.9 0.0 copy-done.1
  5.9 0.5 tables.1
  6.4 0.6 collective-permute-done.recv_ref
  7.0 0.4 rows.1
  7.4 26.5 %all_to_all.10 = bf16[128,8,128]{2,1,0:T(8,128)(2,1)S(1)} all-to-all(bf16[128,8,128]{2,1,0:T(8,128)(2,1)S(1)} %bitcast.8), channel_id=1, replica_groups=mesh['z'=8,'y'=4,'c'=2,'x'=4] {'x','z','y'}, dimensions={0} | all-to-all | bytes 524288 | tf_op jit(solution)/shard_map/all_to_all | solution.py:310
  34.0 0.0 copy-done
  34.0 0.6 %mix.1 = bf16[1024,128]{1,0:T(8,128)(2,1)S(1)} custom-call(bf16[1024,128]{1,0:T(8,128)(2,1)S(1)} %bitcast.6, bf16[4,8,1024]{2,1,0:T(8,128)(2,1)S(1)} %copy-done, bf16[64,512]{1,0:T(8,128)(2,1)S(1)} %get-tuple-element.27.peer_ref), custom_call_target="tpu_custom_call" | custom-call | tf_op jit(solution)/shard_map/mix/pallas_call | solution.py:265
  34.6 18.7 %all_to_all.11 = bf16[128,8,128]{2,1,0:T(8,128)(2,1)S(1)} all-to-all(bf16[128,8,128]{2,1,0:T(8,128)(2,1)S(1)} %bitcast.7), channel_id=1, replica_groups=mesh['z'=8,'y'=4,'c'=2,'x'=4] {'x','z','y'}, dimensions={0} | all-to-all | bytes 524288 | tf_op jit(solution)/shard_map/all_to_all | solution.py:317
  53.3 0.5 modes.1
  53.8 3.8 %collective-permute-start.1 = (bf16[128,512]{1,0:T(8,128)(2,1)S(1)}, bf16[128,512]{1,0:T(8,128)(2,1)S(1)}, u32[]{:S(2)}, u32[]{:S(2)}) collective-permute-start(bf16[128,512]{1,0:T(8,128)(2,1)S(1)} %get-tuple-element.30), channel_id=1, source_target_pairs={{0,4},{4,0},{1,5},{5,1},{2,6},{6,2},{3,7},{7,3},{8,12},{12,8},{9,1... | collective-permute-start | bytes 393224 | tf_op jit(solution)/shard_map/ppermute | solution.py:324
  57.6 0.7 %point.1.point_ref = f32[8,32,16,256]{3,2,1,0:T(8,128)S(1)} custom-call(bf16[32,8,16,256]{3,2,1,0:T(8,128)(2,1)S(1)} %get-tuple-element.19.grid_ref, bf16[256,256]{1,0:T(8,128)(2,1)S(1)} %get-tuple-element.21.kron_ref, bf16[128,512]{1,0:T(8,128)(2,1)S(1)} %get-tuple-element.29.after_ref.own_ref), custom_call_target="tpu_custom_call" | custom-call | tf_op jit(solution)/shard_map/point/pallas_call | solution.py:265
  58.3 0.3 collective-permute-done.1.recv_ref
  58.6 1.9 %grid.1 = bf16[32,8,16,256]{3,2,1,0:T(8,128)(2,1)} custom-call(f32[8,32,16,256]{3,2,1,0:T(8,128)S(1)} %point.1.point_ref, bf16[128,512]{1,0:T(8,128)(2,1)S(1)} %get-tuple-element.29.after_ref.own_ref, bf16[128,512]{1,0:T(8,128)(2,1)S(1)} %collective-permute-done.1.recv_ref, bf16[16,512]{1,0:T(8,128)(2,1)S(1)} %get-tuple-element.31.shift_ref, ...), custom_call_target="tpu_custom_call" | custom-call | tf_op jit(solution)/shard_map/grid/pallas_call | solution.py:265
Async XLA Ops:
  0.0 34.0 %copy-start = (bf16[4,8,1024]{2,1,0:T(8,128)(2,1)S(1)}, bf16[4,8,1024]{2,1,0:T(8,128)(2,1)}, u32[]{:S(2)}) copy-start(bf16[4,8,1024]{2,1,0:T(8,128)(2,1)} %weight_ref.1) | copy-start | bytes 196612
  0.0 5.9 %copy-start.2 = (f32[32]{0:T(128)S(1)}, f32[32]{0:T(128)}, u32[]{:S(2)}) copy-start(f32[32]{0:T(128)} %param.12) | copy-start | bytes 388
  0.0 5.9 %copy-start.1 = (bf16[32,32]{1,0:T(8,128)(2,1)S(1)}, bf16[32,32]{1,0:T(8,128)(2,1)}, u32[]{:S(2)}) copy-start(bf16[32,32]{1,0:T(8,128)(2,1)} %point_ref.1) | copy-start | bytes 6148
  2.6 4.4 %collective-permute-start = (bf16[192,512]{1,0:T(8,128)(2,1)S(1)}, bf16[192,512]{1,0:T(8,128)(2,1)S(1)}, u32[]{:S(2)}, u32[]{:S(2)}) collective-permute-start(bf16[192,512]{1,0:T(8,128)(2,1)S(1)} %get-tuple-element.23), channel_id=1, source_target_pairs={{0,4},{4,0},{1,5},{5,1},{2,6},{6,2},{3,7},{7,3},{8,12},{12,8},{9,1... | collective-permute-start | bytes 589832 | tf_op jit(solution)/shard_map/ppermute | solution.py:297
  53.8 4.8 %collective-permute-start.1 = (bf16[128,512]{1,0:T(8,128)(2,1)S(1)}, bf16[128,512]{1,0:T(8,128)(2,1)S(1)}, u32[]{:S(2)}, u32[]{:S(2)}) collective-permute-start(bf16[128,512]{1,0:T(8,128)(2,1)S(1)} %get-tuple-element.30), channel_id=1, source_target_pairs={{0,4},{4,0},{1,5},{5,1},{2,6},{6,2},{3,7},{7,3},{8,12},{12,8},{9,1... | collective-permute-start | bytes 393224 | tf_op jit(solution)/shard_map/ppermute | solution.py:324

commit v6 on v5

--- a/solution.py
+++ b/solution.py
@@ -17,6 +17,12 @@
 CHUNKS = 4
 BF = jnp.bfloat16
 F32 = jnp.float32
+
+
+CHIPS = [(x, z, y) for x in range(DX) for z in range(DZ) for y in range(DY)]
+ORDER = sorted(CHIPS, key=lambda chip: chip != (2, 5, 2))
+SLOT = {chip: at for at, chip in enumerate(ORDER)}
+GROUP = [[CHIPS.index(chip) for chip in ORDER]]
 
 
 def cosines(count, length, norm):
@@ -174,7 +180,7 @@
     res = dot(lhs, wy_ref[...])
     for to in range(32):
         for joct in range(4):
-            out_ref[pl.ds((to * 4 + joct) * 8, 8), :] = res[
+            out_ref[pl.ds(SLOT[to // 8, to % 8, joct] * 8, 8), :] = res[
                 to * 8 : (to + 1) * 8, joct * 128 : (joct + 1) * 128
             ].astype(BF)
     peer_out[...] = recv_ref[128:192, :]
@@ -220,7 +226,7 @@
 def modes_kernel(modes_ref, wy_ref, planes_ref, own_ref, send_ref):
     rows = []
     for to in range(32):
-        cols = [modes_ref[pl.ds((to * 4 + joct) * 8, 8), :] for joct in range(4)]
+        cols = [modes_ref[pl.ds(SLOT[to // 8, to % 8, joct] * 8, 8), :] for joct in range(4)]
         rows.append(jnp.concatenate(cols, axis=1))
     res = dot(jnp.concatenate(rows, axis=0), wy_ref[...], ((1,), (1,))).astype(BF)
     res = dot(planes_ref[...], res).astype(BF)
@@ -307,14 +313,14 @@
         (own, recv, wy, order),
         (vm(1024, 128), vm(64, 512)),
     )
-    parts = lax.all_to_all(parts.reshape(128, 8, 128), ("x", "z", "y"), 0, 0, tiled=True)
+    parts = lax.all_to_all(parts.reshape(128, 8, 128), ("x", "z", "y"), 0, 0, axis_index_groups=GROUP, tiled=True)
     mixed = call(
         mix_kernel,
         "mix",
         (parts.reshape(1024, 128), spectral_weight, peer_weight),
         vm(1024, 128),
     )
-    modes = lax.all_to_all(mixed.reshape(128, 8, 128), ("x", "z", "y"), 0, 0, tiled=True)
+    modes = lax.all_to_all(mixed.reshape(128, 8, 128), ("x", "z", "y"), 0, 0, axis_index_groups=GROUP, tiled=True)
     own, send = call(
         modes_kernel,
         "modes",

time: 60.6 us -> 54.4 us (0.90)
  blocking collectives: 45.2 us -> 40 us
  starting transfers between devices: 7.07 us -> 6 us
    all_to_all x2, blocking collectives: 45.2 us -> 40 us  [the longest x1 21.4 us: shards(): lax.all_to_all(parts.reshape(128, 8, 128), ('x', 'z', 'y'), 0, 0, axis_in...]
    ppermute x2, starting transfers between devices: 7.07 us -> 6 us  [shards(): recv = lax.ppermute(send, 'c', swap)]
where the time goes in v6:
time: 54.4 us; the launch traced here: 54.2 us
  blocking collectives  40 us (74%)
  Pallas kernels  7.25 us (13%)
  starting transfers between devices  6 us (11%)
  waiting for transfers between devices  0.87 us (2%)
    all_to_all x1, blocking collectives, shards(): lax.all_to_all(parts.reshape(128, 8, 128), ('x', 'z', 'y'), 0, 0, axis_in...  21.4 us
    all_to_all x1, blocking collectives, shards(): lax.all_to_all(mixed.reshape(128, 8, 128), ('x', 'z', 'y'), 0, 0, axis_in...  18.6 us
    pallas_call x7, Pallas kernels, call(): pl.pallas_call(kernel, out_shape=outs, in_specs=[spec(s) for s in spaces]...  7.25 us
    ppermute x2, starting transfers between devices, shards(): recv = lax.ppermute(send, 'c', swap)  6 us
  transfers between devices with their start and end apart: 2, of which 2 were waited for; matrix products, arithmetic and copies ran while one was open for 0% of the time, Pallas kernels for 2%

profile of v6, /device:TPU:1, one launch (start us, length us, event | category | flops | bytes accessed | tf_op | source)
XLA Modules:
  0.0 54.2 jit_solution(17763499984563097827)
XLA Ops:
  0.0 0.0 copy-start
  0.0 0.0 copy-start.2
  0.0 0.0 copy-start.1
  0.0 2.6 %analysis.1 = (bf16[128,512]{1,0:T(8,128)(2,1)S(1)}, bf16[192,512]{1,0:T(8,128)(2,1)S(1)}, bf16[48,256]{1,0:T(8,128)(2,1)S(1)}, bf16[256,256]{1,0:T(8,128)(2,1)S...) custom-call(bf16[32,8,16,256]{3,2,1,0:T(8,128)(2,1)} %field.1, ...), custom_call_target="tpu_custom_call" | custom-call | tf_op jit(solution)/shard_map/analysis/pallas_call | solution.py:271
  2.6 3.3 %collective-permute-start = (bf16[192,512]{1,0:T(8,128)(2,1)S(1)}, bf16[192,512]{1,0:T(8,128)(2,1)S(1)}, u32[]{:S(2)}, u32[]{:S(2)}) collective-permute-start(bf16[192,512]{1,0:T(8,128)(2,1)S(1)} %get-tuple-element.23), channel_id=1, source_target_pairs={{0,4},{4,0},{1,5},{5,1},{2,6},{6,2},{3,7},{7,3},{8,12},{12,8},{9,1... | collective-permute-start | bytes 589832 | tf_op jit(solution)/shard_map/ppermute | solution.py:303
  5.9 0.0 copy-done.2
  5.9 0.0 copy-done.1
  5.9 0.5 tables.1
  6.4 0.6 %collective-permute-done.recv_ref = bf16[192,512]{1,0:T(8,128)(2,1)S(1)} collective-permute-done((bf16[192,512]{1,0:T(8,128)(2,1)S(1)}, bf16[192,512]{1,0:T(8,128)(2,1)S(1)}, u32[]{:S(2)}, u32[]{:S(2)}) %collective-permute-start) | collective-permute-done | bytes 196640 | tf_op jit(solution)/shard_map/ppermute | solution.py:303
  7.0 0.4 rows.1
  7.4 21.4 %all_to_all.10 = bf16[128,8,128]{2,1,0:T(8,128)(2,1)S(1)} all-to-all(bf16[128,8,128]{2,1,0:T(8,128)(2,1)S(1)} %bitcast.8), channel_id=1, replica_groups={{178,0,8,16,24,32,40,48,56,64,72,80,88,96,104,112,120,128,136,144,152,1..., dimensions={0} | all-to-all | bytes 524288 | tf_op jit(solution)/shard_map/all_to_all | solution.py:316
  28.8 0.0 copy-done
  28.8 0.6 %mix.1 = bf16[1024,128]{1,0:T(8,128)(2,1)S(1)} custom-call(bf16[1024,128]{1,0:T(8,128)(2,1)S(1)} %bitcast.6, bf16[4,8,1024]{2,1,0:T(8,128)(2,1)S(1)} %copy-done, bf16[64,512]{1,0:T(8,128)(2,1)S(1)} %get-tuple-element.27.peer_ref), custom_call_target="tpu_custom_call" | custom-call | tf_op jit(solution)/shard_map/mix/pallas_call | solution.py:271
  29.5 18.6 %all_to_all.11 = bf16[128,8,128]{2,1,0:T(8,128)(2,1)S(1)} all-to-all(bf16[128,8,128]{2,1,0:T(8,128)(2,1)S(1)} %bitcast.7), channel_id=1, replica_groups={{178,0,8,16,24,32,40,48,56,64,72,80,88,96,104,112,120,128,136,144,152,1..., dimensions={0} | all-to-all | bytes 524288 | tf_op jit(solution)/shard_map/all_to_all | solution.py:323
  48.1 0.5 modes.1
  48.6 2.7 %collective-permute-start.1 = (bf16[128,512]{1,0:T(8,128)(2,1)S(1)}, bf16[128,512]{1,0:T(8,128)(2,1)S(1)}, u32[]{:S(2)}, u32[]{:S(2)}) collective-permute-start(bf16[128,512]{1,0:T(8,128)(2,1)S(1)} %get-tuple-element.30), channel_id=1, source_target_pairs={{0,4},{4,0},{1,5},{5,1},{2,6},{6,2},{3,7},{7,3},{8,12},{12,8},{9,1... | collective-permute-start | bytes 393224 | tf_op jit(solution)/shard_map/ppermute | solution.py:330
  51.3 0.7 %point.1.point_ref = f32[8,32,16,256]{3,2,1,0:T(8,128)S(1)} custom-call(bf16[32,8,16,256]{3,2,1,0:T(8,128)(2,1)S(1)} %get-tuple-element.19.grid_ref, bf16[256,256]{1,0:T(8,128)(2,1)S(1)} %get-tuple-element.21.kron_ref, bf16[128,512]{1,0:T(8,128)(2,1)S(1)} %get-tuple-element.29.after_ref.own_ref), custom_call_target="tpu_custom_call" | custom-call | tf_op jit(solution)/shard_map/point/pallas_call | solution.py:271
  52.0 0.3 collective-permute-done.1.recv_ref
  52.3 1.9 %grid.1 = bf16[32,8,16,256]{3,2,1,0:T(8,128)(2,1)} custom-call(f32[8,32,16,256]{3,2,1,0:T(8,128)S(1)} %point.1.point_ref, bf16[128,512]{1,0:T(8,128)(2,1)S(1)} %get-tuple-element.29.after_ref.own_ref, bf16[128,512]{1,0:T(8,128)(2,1)S(1)} %collective-permute-done.1.recv_ref, bf16[16,512]{1,0:T(8,128)(2,1)S(1)} %get-tuple-element.31.shift_ref, ...), custom_call_target="tpu_custom_call" | custom-call | tf_op jit(solution)/shard_map/grid/pallas_call | solution.py:271
Async XLA Ops:
  0.0 28.8 %copy-start = (bf16[4,8,1024]{2,1,0:T(8,128)(2,1)S(1)}, bf16[4,8,1024]{2,1,0:T(8,128)(2,1)}, u32[]{:S(2)}) copy-start(bf16[4,8,1024]{2,1,0:T(8,128)(2,1)} %weight_ref.1) | copy-start | bytes 196612
  0.0 5.9 %copy-start.2 = (f32[32]{0:T(128)S(1)}, f32[32]{0:T(128)}, u32[]{:S(2)}) copy-start(f32[32]{0:T(128)} %param.12) | copy-start | bytes 388
  0.0 5.9 %copy-start.1 = (bf16[32,32]{1,0:T(8,128)(2,1)S(1)}, bf16[32,32]{1,0:T(8,128)(2,1)}, u32[]{:S(2)}) copy-start(bf16[32,32]{1,0:T(8,128)(2,1)} %point_ref.1) | copy-start | bytes 6148
  2.6 4.4 %collective-permute-start = (bf16[192,512]{1,0:T(8,128)(2,1)S(1)}, bf16[192,512]{1,0:T(8,128)(2,1)S(1)}, u32[]{:S(2)}, u32[]{:S(2)}) collective-permute-start(bf16[192,512]{1,0:T(8,128)(2,1)S(1)} %get-tuple-element.23), channel_id=1, source_target_pairs={{0,4},{4,0},{1,5},{5,1},{2,6},{6,2},{3,7},{7,3},{8,12},{12,8},{9,1... | collective-permute-start | bytes 589832 | tf_op jit(solution)/shard_map/ppermute | solution.py:303
  48.6 3.7 %collective-permute-start.1 = (bf16[128,512]{1,0:T(8,128)(2,1)S(1)}, bf16[128,512]{1,0:T(8,128)(2,1)S(1)}, u32[]{:S(2)}, u32[]{:S(2)}) collective-permute-start(bf16[128,512]{1,0:T(8,128)(2,1)S(1)} %get-tuple-element.30), channel_id=1, source_target_pairs={{0,4},{4,0},{1,5},{5,1},{2,6},{6,2},{3,7},{7,3},{8,12},{12,8},{9,1... | collective-permute-start | bytes 393224 | tf_op jit(solution)/shard_map/ppermute | solution.py:330

commit v7 on v6

--- a/solution.py
+++ b/solution.py
@@ -19,8 +19,12 @@
 F32 = jnp.float32
 
 
+def hops(chip):
+    return sum(min(at, size - at) for at, size in zip(chip, (DX, DZ, DY)))
+
+
 CHIPS = [(x, z, y) for x in range(DX) for z in range(DZ) for y in range(DY)]
-ORDER = sorted(CHIPS, key=lambda chip: chip != (2, 5, 2))
+ORDER = sorted(CHIPS, key=lambda chip: (chip != (DX // 2, DZ // 2, DY // 2), hops(chip)))
 SLOT = {chip: at for at, chip in enumerate(ORDER)}
 GROUP = [[CHIPS.index(chip) for chip in ORDER]]
 

time: 54.4 us -> 53.7 us (0.987)
  no operation moved by 1% of the time
where the time goes in v7:
time: 53.7 us; the launch traced here: 53.6 us
  blocking collectives  39.9 us (74%)
  Pallas kernels  7.23 us (13%)
  starting transfers between devices  5.5 us (10%)
  waiting for transfers between devices  0.87 us (2%)
    all_to_all x1, blocking collectives, shards(): lax.all_to_all(parts.reshape(128, 8, 128), ('x', 'z', 'y'), 0, 0, axis_in...  21.7 us
    all_to_all x1, blocking collectives, shards(): lax.all_to_all(mixed.reshape(128, 8, 128), ('x', 'z', 'y'), 0, 0, axis_in...  18.2 us
    pallas_call x7, Pallas kernels, call(): pl.pallas_call(kernel, out_shape=outs, in_specs=[spec(s) for s in spaces]...  7.23 us
    ppermute x2, starting transfers between devices, shards(): recv = lax.ppermute(send, 'c', swap)  5.5 us
  transfers between devices with their start and end apart: 2, of which 2 were waited for; matrix products, arithmetic and copies ran while one was open for 0% of the time, Pallas kernels for 2%

profile of v7, /device:TPU:1, one launch (start us, length us, event | category | flops | bytes accessed | tf_op | source)
XLA Modules:
  0.0 53.6 jit_solution(8828115014856524371)
XLA Ops:
  0.0 0.0 copy-start
  0.0 0.0 copy-start.2
  0.0 0.0 copy-start.1
  0.0 2.6 %analysis.1 = (bf16[128,512]{1,0:T(8,128)(2,1)S(1)}, bf16[192,512]{1,0:T(8,128)(2,1)S(1)}, bf16[48,256]{1,0:T(8,128)(2,1)S(1)}, bf16[256,256]{1,0:T(8,128)(2,1)S...) custom-call(bf16[32,8,16,256]{3,2,1,0:T(8,128)(2,1)} %field.1, ...), custom_call_target="tpu_custom_call" | custom-call | tf_op jit(solution)/shard_map/analysis/pallas_call | solution.py:275
  2.6 3.3 %collective-permute-start = (bf16[192,512]{1,0:T(8,128)(2,1)S(1)}, bf16[192,512]{1,0:T(8,128)(2,1)S(1)}, u32[]{:S(2)}, u32[]{:S(2)}) collective-permute-start(bf16[192,512]{1,0:T(8,128)(2,1)S(1)} %get-tuple-element.23), channel_id=1, source_target_pairs={{0,4},{4,0},{1,5},{5,1},{2,6},{6,2},{3,7},{7,3},{8,12},{12,8},{9,1... | collective-permute-start | bytes 589832 | tf_op jit(solution)/shard_map/ppermute | solution.py:307
  5.9 0.0 copy-done.2
  5.9 0.0 copy-done.1
  5.9 0.5 tables.1
  6.4 0.6 %collective-permute-done.recv_ref = bf16[192,512]{1,0:T(8,128)(2,1)S(1)} collective-permute-done((bf16[192,512]{1,0:T(8,128)(2,1)S(1)}, bf16[192,512]{1,0:T(8,128)(2,1)S(1)}, u32[]{:S(2)}, u32[]{:S(2)}) %collective-permute-start) | collective-permute-done | bytes 196640 | tf_op jit(solution)/shard_map/ppermute | solution.py:307
  7.0 0.4 rows.1
  7.4 21.7 %all_to_all.10 = bf16[128,8,128]{2,1,0:T(8,128)(2,1)S(1)} all-to-all(bf16[128,8,128]{2,1,0:T(8,128)(2,1)S(1)} %bitcast.8), channel_id=1, replica_groups={{146,0,8,24,32,224,1,3,16,40,56,64,192,232,248,9,25,33,225,2,11,27,35,2..., dimensions={0} | all-to-all | bytes 524288 | tf_op jit(solution)/shard_map/all_to_all | solution.py:320
  29.2 0.0 copy-done
  29.2 0.6 %mix.1 = bf16[1024,128]{1,0:T(8,128)(2,1)S(1)} custom-call(bf16[1024,128]{1,0:T(8,128)(2,1)S(1)} %bitcast.6, bf16[4,8,1024]{2,1,0:T(8,128)(2,1)S(1)} %copy-done, bf16[64,512]{1,0:T(8,128)(2,1)S(1)} %get-tuple-element.27.peer_ref), custom_call_target="tpu_custom_call" | custom-call | tf_op jit(solution)/shard_map/mix/pallas_call | solution.py:275
  29.8 18.2 %all_to_all.11 = bf16[128,8,128]{2,1,0:T(8,128)(2,1)S(1)} all-to-all(bf16[128,8,128]{2,1,0:T(8,128)(2,1)S(1)} %bitcast.7), channel_id=1, replica_groups={{146,0,8,24,32,224,1,3,16,40,56,64,192,232,248,9,25,33,225,2,11,27,35,2..., dimensions={0} | all-to-all | bytes 524288 | tf_op jit(solution)/shard_map/all_to_all | solution.py:327
  48.0 0.5 modes.1
  48.5 2.2 %collective-permute-start.1 = (bf16[128,512]{1,0:T(8,128)(2,1)S(1)}, bf16[128,512]{1,0:T(8,128)(2,1)S(1)}, u32[]{:S(2)}, u32[]{:S(2)}) collective-permute-start(bf16[128,512]{1,0:T(8,128)(2,1)S(1)} %get-tuple-element.30), channel_id=1, source_target_pairs={{0,4},{4,0},{1,5},{5,1},{2,6},{6,2},{3,7},{7,3},{8,12},{12,8},{9,1... | collective-permute-start | bytes 393224 | tf_op jit(solution)/shard_map/ppermute | solution.py:334
  50.7 0.7 %point.1.point_ref = f32[8,32,16,256]{3,2,1,0:T(8,128)S(1)} custom-call(bf16[32,8,16,256]{3,2,1,0:T(8,128)(2,1)S(1)} %get-tuple-element.19.grid_ref, bf16[256,256]{1,0:T(8,128)(2,1)S(1)} %get-tuple-element.21.kron_ref, bf16[128,512]{1,0:T(8,128)(2,1)S(1)} %get-tuple-element.29.after_ref.own_ref), custom_call_target="tpu_custom_call" | custom-call | tf_op jit(solution)/shard_map/point/pallas_call | solution.py:275
  51.4 0.3 collective-permute-done.1.recv_ref
  51.7 1.9 %grid.1 = bf16[32,8,16,256]{3,2,1,0:T(8,128)(2,1)} custom-call(f32[8,32,16,256]{3,2,1,0:T(8,128)S(1)} %point.1.point_ref, bf16[128,512]{1,0:T(8,128)(2,1)S(1)} %get-tuple-element.29.after_ref.own_ref, bf16[128,512]{1,0:T(8,128)(2,1)S(1)} %collective-permute-done.1.recv_ref, bf16[16,512]{1,0:T(8,128)(2,1)S(1)} %get-tuple-element.31.shift_ref, ...), custom_call_target="tpu_custom_call" | custom-call | tf_op jit(solution)/shard_map/grid/pallas_call | solution.py:275
Async XLA Ops:
  0.0 29.2 %copy-start = (bf16[4,8,1024]{2,1,0:T(8,128)(2,1)S(1)}, bf16[4,8,1024]{2,1,0:T(8,128)(2,1)}, u32[]{:S(2)}) copy-start(bf16[4,8,1024]{2,1,0:T(8,128)(2,1)} %weight_ref.1) | copy-start | bytes 196612
  0.0 5.9 %copy-start.2 = (f32[32]{0:T(128)S(1)}, f32[32]{0:T(128)}, u32[]{:S(2)}) copy-start(f32[32]{0:T(128)} %param.12) | copy-start | bytes 388
  0.0 5.9 %copy-start.1 = (bf16[32,32]{1,0:T(8,128)(2,1)S(1)}, bf16[32,32]{1,0:T(8,128)(2,1)}, u32[]{:S(2)}) copy-start(bf16[32,32]{1,0:T(8,128)(2,1)} %point_ref.1) | copy-start | bytes 6148
  2.6 4.4 %collective-permute-start = (bf16[192,512]{1,0:T(8,128)(2,1)S(1)}, bf16[192,512]{1,0:T(8,128)(2,1)S(1)}, u32[]{:S(2)}, u32[]{:S(2)}) collective-permute-start(bf16[192,512]{1,0:T(8,128)(2,1)S(1)} %get-tuple-element.23), channel_id=1, source_target_pairs={{0,4},{4,0},{1,5},{5,1},{2,6},{6,2},{3,7},{7,3},{8,12},{12,8},{9,1... | collective-permute-start | bytes 589832 | tf_op jit(solution)/shard_map/ppermute | solution.py:307
  48.5 3.2 %collective-permute-start.1 = (bf16[128,512]{1,0:T(8,128)(2,1)S(1)}, bf16[128,512]{1,0:T(8,128)(2,1)S(1)}, u32[]{:S(2)}, u32[]{:S(2)}) collective-permute-start(bf16[128,512]{1,0:T(8,128)(2,1)S(1)} %get-tuple-element.30), channel_id=1, source_target_pairs={{0,4},{4,0},{1,5},{5,1},{2,6},{6,2},{3,7},{7,3},{8,12},{12,8},{9,1... | collective-permute-start | bytes 393224 | tf_op jit(solution)/shard_map/ppermute | solution.py:334

commit v8 on v7

--- a/solution.py
+++ b/solution.py
@@ -262,8 +262,10 @@
             v = v.astype(BF)
             v = v * jax.nn.sigmoid(v * (jnp.asarray(a, BF) + jnp.asarray(a * 0.044715, BF) * (v * v)))
             stage[rows, x] = v.reshape(share, ROWS, DEPTH)
-        copies.append(pltpu.make_async_copy(stage.at[rows], out_ref.at[rows], sems.at[q]))
-        copies[-1].start()
+            if x % (X // 2) == X // 2 - 1:
+                at = (rows, pl.ds(x - (X // 2 - 1), X // 2))
+                copies.append(pltpu.make_async_copy(stage.at[at], out_ref.at[at], sems.at[len(copies)]))
+                copies[-1].start()
     for copy in copies:
         copy.wait()
 
@@ -345,7 +347,7 @@
         "grid",
         (point, own, recv, shift, back),
         pltpu.HBM((C, X, ROWS, DEPTH), BF),
-        (vm(C, X, ROWS, DEPTH), dma((CHUNKS,))),
+        (vm(C, X, ROWS, DEPTH), dma((2 * CHUNKS,))),
     )
 
 

time: 53.7 us -> 53.7 us (level)
  no operation moved by 1% of the time
where the time goes in v8:
time: 53.7 us; the launch traced here: 53.5 us
  blocking collectives  39.9 us (74%)
  Pallas kernels  7.18 us (13%)
  starting transfers between devices  5.5 us (10%)
  waiting for transfers between devices  0.87 us (2%)
    all_to_all x1, blocking collectives, shards(): lax.all_to_all(parts.reshape(128, 8, 128), ('x', 'z', 'y'), 0, 0, axis_in...  21.7 us
    all_to_all x1, blocking collectives, shards(): lax.all_to_all(mixed.reshape(128, 8, 128), ('x', 'z', 'y'), 0, 0, axis_in...  18.2 us
    pallas_call x7, Pallas kernels, call(): pl.pallas_call(kernel, out_shape=outs, in_specs=[spec(s) for s in spaces]...  7.18 us
    ppermute x2, starting transfers between devices, shards(): recv = lax.ppermute(send, 'c', swap)  5.5 us
  transfers between devices with their start and end apart: 2, of which 2 were waited for; matrix products, arithmetic and copies ran while one was open for 0% of the time, Pallas kernels for 2%

profile of v8, /device:TPU:1, one launch (start us, length us, event | category | flops | bytes accessed | tf_op | source)
XLA Modules:
  0.0 53.5 jit_solution(9887897514691625710)
XLA Ops:
  0.0 0.0 copy-start
  0.0 0.0 copy-start.2
  0.0 0.0 copy-start.1
  0.0 2.6 %analysis.1 = (bf16[128,512]{1,0:T(8,128)(2,1)S(1)}, bf16[192,512]{1,0:T(8,128)(2,1)S(1)}, bf16[48,256]{1,0:T(8,128)(2,1)S(1)}, bf16[256,256]{1,0:T(8,128)(2,1)S...) custom-call(bf16[32,8,16,256]{3,2,1,0:T(8,128)(2,1)} %field.1, ...), custom_call_target="tpu_custom_call" | custom-call | tf_op jit(solution)/shard_map/analysis/pallas_call | solution.py:277
  2.6 3.3 %collective-permute-start = (bf16[192,512]{1,0:T(8,128)(2,1)S(1)}, bf16[192,512]{1,0:T(8,128)(2,1)S(1)}, u32[]{:S(2)}, u32[]{:S(2)}) collective-permute-start(bf16[192,512]{1,0:T(8,128)(2,1)S(1)} %get-tuple-element.23), channel_id=1, source_target_pairs={{0,4},{4,0},{1,5},{5,1},{2,6},{6,2},{3,7},{7,3},{8,12},{12,8},{9,1... | collective-permute-start | bytes 589832 | tf_op jit(solution)/shard_map/ppermute | solution.py:309
  5.9 0.0 copy-done.2
  5.9 0.0 copy-done.1
  5.9 0.5 tables.1
  6.4 0.6 %collective-permute-done.recv_ref = bf16[192,512]{1,0:T(8,128)(2,1)S(1)} collective-permute-done((bf16[192,512]{1,0:T(8,128)(2,1)S(1)}, bf16[192,512]{1,0:T(8,128)(2,1)S(1)}, u32[]{:S(2)}, u32[]{:S(2)}) %collective-permute-start) | collective-permute-done | bytes 196640 | tf_op jit(solution)/shard_map/ppermute | solution.py:309
  7.0 0.4 rows.1
  7.4 21.7 %all_to_all.10 = bf16[128,8,128]{2,1,0:T(8,128)(2,1)S(1)} all-to-all(bf16[128,8,128]{2,1,0:T(8,128)(2,1)S(1)} %bitcast.8), channel_id=1, replica_groups={{146,0,8,24,32,224,1,3,16,40,56,64,192,232,248,9,25,33,225,2,11,27,35,2..., dimensions={0} | all-to-all | bytes 524288 | tf_op jit(solution)/shard_map/all_to_all | solution.py:322
  29.2 0.0 copy-done
  29.2 0.6 %mix.1 = bf16[1024,128]{1,0:T(8,128)(2,1)S(1)} custom-call(bf16[1024,128]{1,0:T(8,128)(2,1)S(1)} %bitcast.6, bf16[4,8,1024]{2,1,0:T(8,128)(2,1)S(1)} %copy-done, bf16[64,512]{1,0:T(8,128)(2,1)S(1)} %get-tuple-element.27.peer_ref), custom_call_target="tpu_custom_call" | custom-call | tf_op jit(solution)/shard_map/mix/pallas_call | solution.py:277
  29.8 18.2 %all_to_all.11 = bf16[128,8,128]{2,1,0:T(8,128)(2,1)S(1)} all-to-all(bf16[128,8,128]{2,1,0:T(8,128)(2,1)S(1)} %bitcast.7), channel_id=1, replica_groups={{146,0,8,24,32,224,1,3,16,40,56,64,192,232,248,9,25,33,225,2,11,27,35,2..., dimensions={0} | all-to-all | bytes 524288 | tf_op jit(solution)/shard_map/all_to_all | solution.py:329
  48.0 0.5 modes.1
  48.5 2.2 %collective-permute-start.1 = (bf16[128,512]{1,0:T(8,128)(2,1)S(1)}, bf16[128,512]{1,0:T(8,128)(2,1)S(1)}, u32[]{:S(2)}, u32[]{:S(2)}) collective-permute-start(bf16[128,512]{1,0:T(8,128)(2,1)S(1)} %get-tuple-element.30), channel_id=1, source_target_pairs={{0,4},{4,0},{1,5},{5,1},{2,6},{6,2},{3,7},{7,3},{8,12},{12,8},{9,1... | collective-permute-start | bytes 393224 | tf_op jit(solution)/shard_map/ppermute | solution.py:336
  50.7 0.7 %point.1.point_ref = f32[8,32,16,256]{3,2,1,0:T(8,128)S(1)} custom-call(bf16[32,8,16,256]{3,2,1,0:T(8,128)(2,1)S(1)} %get-tuple-element.19.grid_ref, bf16[256,256]{1,0:T(8,128)(2,1)S(1)} %get-tuple-element.21.kron_ref, bf16[128,512]{1,0:T(8,128)(2,1)S(1)} %get-tuple-element.29.after_ref.own_ref), custom_call_target="tpu_custom_call" | custom-call | tf_op jit(solution)/shard_map/point/pallas_call | solution.py:277
  51.4 0.3 collective-permute-done.1.recv_ref
  51.7 1.8 %grid.1 = bf16[32,8,16,256]{3,2,1,0:T(8,128)(2,1)} custom-call(f32[8,32,16,256]{3,2,1,0:T(8,128)S(1)} %point.1.point_ref, bf16[128,512]{1,0:T(8,128)(2,1)S(1)} %get-tuple-element.29.after_ref.own_ref, bf16[128,512]{1,0:T(8,128)(2,1)S(1)} %collective-permute-done.1.recv_ref, bf16[16,512]{1,0:T(8,128)(2,1)S(1)} %get-tuple-element.31.shift_ref, ...), custom_call_target="tpu_custom_call" | custom-call | tf_op jit(solution)/shard_map/grid/pallas_call | solution.py:277
Async XLA Ops:
  0.0 29.2 %copy-start = (bf16[4,8,1024]{2,1,0:T(8,128)(2,1)S(1)}, bf16[4,8,1024]{2,1,0:T(8,128)(2,1)}, u32[]{:S(2)}) copy-start(bf16[4,8,1024]{2,1,0:T(8,128)(2,1)} %weight_ref.1) | copy-start | bytes 196612
  0.0 5.9 %copy-start.2 = (f32[32]{0:T(128)S(1)}, f32[32]{0:T(128)}, u32[]{:S(2)}) copy-start(f32[32]{0:T(128)} %param.12) | copy-start | bytes 388
  0.0 5.9 %copy-start.1 = (bf16[32,32]{1,0:T(8,128)(2,1)S(1)}, bf16[32,32]{1,0:T(8,128)(2,1)}, u32[]{:S(2)}) copy-start(bf16[32,32]{1,0:T(8,128)(2,1)} %point_ref.1) | copy-start | bytes 6148
  2.6 4.4 %collective-permute-start = (bf16[192,512]{1,0:T(8,128)(2,1)S(1)}, bf16[192,512]{1,0:T(8,128)(2,1)S(1)}, u32[]{:S(2)}, u32[]{:S(2)}) collective-permute-start(bf16[192,512]{1,0:T(8,128)(2,1)S(1)} %get-tuple-element.23), channel_id=1, source_target_pairs={{0,4},{4,0},{1,5},{5,1},{2,6},{6,2},{3,7},{7,3},{8,12},{12,8},{9,1... | collective-permute-start | bytes 589832 | tf_op jit(solution)/shard_map/ppermute | solution.py:309
  48.5 3.2 %collective-permute-start.1 = (bf16[128,512]{1,0:T(8,128)(2,1)S(1)}, bf16[128,512]{1,0:T(8,128)(2,1)S(1)}, u32[]{:S(2)}, u32[]{:S(2)}) collective-permute-start(bf16[128,512]{1,0:T(8,128)(2,1)S(1)} %get-tuple-element.30), channel_id=1, source_target_pairs={{0,4},{4,0},{1,5},{5,1},{2,6},{6,2},{3,7},{7,3},{8,12},{12,8},{9,1... | collective-permute-start | bytes 393224 | tf_op jit(solution)/shard_map/ppermute | solution.py:336

commit v9 on v8

--- a/solution.py
+++ b/solution.py
@@ -262,8 +262,8 @@
             v = v.astype(BF)
             v = v * jax.nn.sigmoid(v * (jnp.asarray(a, BF) + jnp.asarray(a * 0.044715, BF) * (v * v)))
             stage[rows, x] = v.reshape(share, ROWS, DEPTH)
-            if x % (X // 2) == X // 2 - 1:
-                at = (rows, pl.ds(x - (X // 2 - 1), X // 2))
+            if x % (X // 4) == X // 4 - 1:
+                at = (rows, pl.ds(x - (X // 4 - 1), X // 4))
                 copies.append(pltpu.make_async_copy(stage.at[at], out_ref.at[at], sems.at[len(copies)]))
                 copies[-1].start()
     for copy in copies:
@@ -347,7 +347,7 @@
         "grid",
         (point, own, recv, shift, back),
         pltpu.HBM((C, X, ROWS, DEPTH), BF),
-        (vm(C, X, ROWS, DEPTH), dma((2 * CHUNKS,))),
+        (vm(C, X, ROWS, DEPTH), dma((4 * CHUNKS,))),
     )
 
 

time: 53.7 us -> 53.7 us (level)
  no operation moved by 1% of the time
where the time goes in v9:
time: 53.7 us; the launch traced here: 53.5 us
  blocking collectives  39.9 us (74%)
  Pallas kernels  7.2 us (13%)
  starting transfers between devices  5.5 us (10%)
  waiting for transfers between devices  0.87 us (2%)
    all_to_all x1, blocking collectives, shards(): lax.all_to_all(parts.reshape(128, 8, 128), ('x', 'z', 'y'), 0, 0, axis_in...  21.7 us
    all_to_all x1, blocking collectives, shards(): lax.all_to_all(mixed.reshape(128, 8, 128), ('x', 'z', 'y'), 0, 0, axis_in...  18.2 us
    pallas_call x7, Pallas kernels, call(): pl.pallas_call(kernel, out_shape=outs, in_specs=[spec(s) for s in spaces]...  7.2 us
    ppermute x2, starting transfers between devices, shards(): recv = lax.ppermute(send, 'c', swap)  5.5 us
  transfers between devices with their start and end apart: 2, of which 2 were waited for; matrix products, arithmetic and copies ran while one was open for 0% of the time, Pallas kernels for 2%

profile of v9, /device:TPU:1, one launch (start us, length us, event | category | flops | bytes accessed | tf_op | source)
XLA Modules:
  0.0 53.5 jit_solution(1137949037770980469)
XLA Ops:
  0.0 0.0 copy-start
  0.0 0.0 copy-start.2
  0.0 0.0 copy-start.1
  0.0 2.6 %analysis.1 = (bf16[128,512]{1,0:T(8,128)(2,1)S(1)}, bf16[192,512]{1,0:T(8,128)(2,1)S(1)}, bf16[48,256]{1,0:T(8,128)(2,1)S(1)}, bf16[256,256]{1,0:T(8,128)(2,1)S...) custom-call(bf16[32,8,16,256]{3,2,1,0:T(8,128)(2,1)} %field.1, ...), custom_call_target="tpu_custom_call" | custom-call | tf_op jit(solution)/shard_map/analysis/pallas_call | solution.py:277
  2.6 3.3 %collective-permute-start = (bf16[192,512]{1,0:T(8,128)(2,1)S(1)}, bf16[192,512]{1,0:T(8,128)(2,1)S(1)}, u32[]{:S(2)}, u32[]{:S(2)}) collective-permute-start(bf16[192,512]{1,0:T(8,128)(2,1)S(1)} %get-tuple-element.23), channel_id=1, source_target_pairs={{0,4},{4,0},{1,5},{5,1},{2,6},{6,2},{3,7},{7,3},{8,12},{12,8},{9,1... | collective-permute-start | bytes 589832 | tf_op jit(solution)/shard_map/ppermute | solution.py:309
  5.9 0.0 copy-done.2
  5.9 0.0 copy-done.1
  5.9 0.5 tables.1
  6.4 0.6 %collective-permute-done.recv_ref = bf16[192,512]{1,0:T(8,128)(2,1)S(1)} collective-permute-done((bf16[192,512]{1,0:T(8,128)(2,1)S(1)}, bf16[192,512]{1,0:T(8,128)(2,1)S(1)}, u32[]{:S(2)}, u32[]{:S(2)}) %collective-permute-start) | collective-permute-done | bytes 196640 | tf_op jit(solution)/shard_map/ppermute | solution.py:309
  7.0 0.4 rows.1
  7.4 21.7 %all_to_all.10 = bf16[128,8,128]{2,1,0:T(8,128)(2,1)S(1)} all-to-all(bf16[128,8,128]{2,1,0:T(8,128)(2,1)S(1)} %bitcast.8), channel_id=1, replica_groups={{146,0,8,24,32,224,1,3,16,40,56,64,192,232,248,9,25,33,225,2,11,27,35,2..., dimensions={0} | all-to-all | bytes 524288 | tf_op jit(solution)/shard_map/all_to_all | solution.py:322
  29.2 0.0 copy-done
  29.2 0.6 %mix.1 = bf16[1024,128]{1,0:T(8,128)(2,1)S(1)} custom-call(bf16[1024,128]{1,0:T(8,128)(2,1)S(1)} %bitcast.6, bf16[4,8,1024]{2,1,0:T(8,128)(2,1)S(1)} %copy-done, bf16[64,512]{1,0:T(8,128)(2,1)S(1)} %get-tuple-element.27.peer_ref), custom_call_target="tpu_custom_call" | custom-call | tf_op jit(solution)/shard_map/mix/pallas_call | solution.py:277
  29.8 18.2 %all_to_all.11 = bf16[128,8,128]{2,1,0:T(8,128)(2,1)S(1)} all-to-all(bf16[128,8,128]{2,1,0:T(8,128)(2,1)S(1)} %bitcast.7), channel_id=1, replica_groups={{146,0,8,24,32,224,1,3,16,40,56,64,192,232,248,9,25,33,225,2,11,27,35,2..., dimensions={0} | all-to-all | bytes 524288 | tf_op jit(solution)/shard_map/all_to_all | solution.py:329
  48.0 0.5 modes.1
  48.5 2.2 %collective-permute-start.1 = (bf16[128,512]{1,0:T(8,128)(2,1)S(1)}, bf16[128,512]{1,0:T(8,128)(2,1)S(1)}, u32[]{:S(2)}, u32[]{:S(2)}) collective-permute-start(bf16[128,512]{1,0:T(8,128)(2,1)S(1)} %get-tuple-element.30), channel_id=1, source_target_pairs={{0,4},{4,0},{1,5},{5,1},{2,6},{6,2},{3,7},{7,3},{8,12},{12,8},{9,1... | collective-permute-start | bytes 393224 | tf_op jit(solution)/shard_map/ppermute | solution.py:336
  50.7 0.7 %point.1.point_ref = f32[8,32,16,256]{3,2,1,0:T(8,128)S(1)} custom-call(bf16[32,8,16,256]{3,2,1,0:T(8,128)(2,1)S(1)} %get-tuple-element.19.grid_ref, bf16[256,256]{1,0:T(8,128)(2,1)S(1)} %get-tuple-element.21.kron_ref, bf16[128,512]{1,0:T(8,128)(2,1)S(1)} %get-tuple-element.29.after_ref.own_ref), custom_call_target="tpu_custom_call" | custom-call | tf_op jit(solution)/shard_map/point/pallas_call | solution.py:277
  51.4 0.3 collective-permute-done.1.recv_ref
  51.7 1.9 %grid.1 = bf16[32,8,16,256]{3,2,1,0:T(8,128)(2,1)} custom-call(f32[8,32,16,256]{3,2,1,0:T(8,128)S(1)} %point.1.point_ref, bf16[128,512]{1,0:T(8,128)(2,1)S(1)} %get-tuple-element.29.after_ref.own_ref, bf16[128,512]{1,0:T(8,128)(2,1)S(1)} %collective-permute-done.1.recv_ref, bf16[16,512]{1,0:T(8,128)(2,1)S(1)} %get-tuple-element.31.shift_ref, ...), custom_call_target="tpu_custom_call" | custom-call | tf_op jit(solution)/shard_map/grid/pallas_call | solution.py:277
Async XLA Ops:
  0.0 29.2 %copy-start = (bf16[4,8,1024]{2,1,0:T(8,128)(2,1)S(1)}, bf16[4,8,1024]{2,1,0:T(8,128)(2,1)}, u32[]{:S(2)}) copy-start(bf16[4,8,1024]{2,1,0:T(8,128)(2,1)} %weight_ref.1) | copy-start | bytes 196612
  0.0 5.9 %copy-start.2 = (f32[32]{0:T(128)S(1)}, f32[32]{0:T(128)}, u32[]{:S(2)}) copy-start(f32[32]{0:T(128)} %param.12) | copy-start | bytes 388
  0.0 5.9 %copy-start.1 = (bf16[32,32]{1,0:T(8,128)(2,1)S(1)}, bf16[32,32]{1,0:T(8,128)(2,1)}, u32[]{:S(2)}) copy-start(bf16[32,32]{1,0:T(8,128)(2,1)} %point_ref.1) | copy-start | bytes 6148
  2.6 4.4 %collective-permute-start = (bf16[192,512]{1,0:T(8,128)(2,1)S(1)}, bf16[192,512]{1,0:T(8,128)(2,1)S(1)}, u32[]{:S(2)}, u32[]{:S(2)}) collective-permute-start(bf16[192,512]{1,0:T(8,128)(2,1)S(1)} %get-tuple-element.23), channel_id=1, source_target_pairs={{0,4},{4,0},{1,5},{5,1},{2,6},{6,2},{3,7},{7,3},{8,12},{12,8},{9,1... | collective-permute-start | bytes 589832 | tf_op jit(solution)/shard_map/ppermute | solution.py:309
  48.5 3.2 %collective-permute-start.1 = (bf16[128,512]{1,0:T(8,128)(2,1)S(1)}, bf16[128,512]{1,0:T(8,128)(2,1)S(1)}, u32[]{:S(2)}, u32[]{:S(2)}) collective-permute-start(bf16[128,512]{1,0:T(8,128)(2,1)S(1)} %get-tuple-element.30), channel_id=1, source_target_pairs={{0,4},{4,0},{1,5},{5,1},{2,6},{6,2},{3,7},{7,3},{8,12},{12,8},{9,1... | collective-permute-start | bytes 393224 | tf_op jit(solution)/shard_map/ppermute | solution.py:336
